TPU v7x, 32 devices: a whole 2x2x4 slice. The times are simulated.
32 devices in a mesh: group: 2 (over y), gx: 4 (over z), gz: 2 (over x), col: 2 (over core).
Axes of the slice: x: 2, y: 2, z: 4, core: 2. Of those that a mesh axis runs over, the one named last changes fastest.
Arguments:
- features: bfloat16 [32, 64, 16, 256], P(None, 'col', ('group', 'gx'), 'gz'), parts along dimension 2, may hold values from -6 to 6
- labels: int32 [64, 16, 256], P(None, ('group', 'gx'), 'gz'), parts along dimension 1, may hold values from 0 to 3
- grid_index: int32 [64], replicated, may hold values from 0 to 15
- stretch: float32 [16, 9], replicated, may hold values from 0.5 to 2
- tile_filter: float32 [32, 25], replicated, may hold values from -1.25 to 1.25
- wall_filter: float32 [32, 9], replicated, may hold values from -2 to 2
- class_weight: float32 [4, 32], replicated, may hold values from -1 to 1
Outputs:
- grad_features: bfloat16 [32, 64, 16, 256], P(None, 'col', ('group', 'gx'), 'gz'), parts along dimension 2
- grad_tile_filter: float32 [64, 25], P('group'), parts along dimension 0
- grad_wall_filter: float32 [64, 9], P('group'), parts along dimension 0
- grad_class_weight: float32 [8, 32], P('group'), parts along dimension 0
There are 2 independent parts, one for each index of `group`. A program takes and returns all parts, laid end to end along the dimension named above; an argument that names none is the same for every part. Nothing has to cross between parts.
All inputs are finite; a program needn't handle non-finite values.
Results may differ from a plain program's by a relative error of at most 0.0064.
Values may be sent and summed in bfloat16 or wider, within the bound.
A program may use at most 64 MiB of HBM per device.

v0:
```python
import functools

import jax
import jax.numpy as jnp
from jax import lax
from jax.experimental import pallas as pl
from jax.experimental.pallas import tpu as pltpu
from jax.sharding import PartitionSpec as P

F32 = jnp.float32
BF16 = jnp.bfloat16
MESH = pl.DeviceIdType.MESH


def fold(value):
    total = value[0:8]
    for row in range(8, value.shape[0], 8):
        total = total + value[row : row + 8]
    return total


def rounded(value):
    return value.astype(BF16).astype(F32)


def kernel(
    dims,
    feat, labels, bands, tile_w, wall_w, class_w,
    out, tile_out, wall_out, class_out,
    recv, band_pad, halo_out, halo_in, zfeat, smooth, stage, taps, band_rows, hid, slope,
    part_own, part_out, part_in, err, gwall, gsm, ghalo_out, ghalo_in, zgrad, gout, gstage,
    acc, red, sums,
    a_send, a_recv, own_sem, h_send, h_recv, s_send, s_recv, p_send, p_recv, e_send, e_recv,
    w_send, w_recv, g_send, g_recv, o_send, o_recv, r_send, r_recv,
):
    size, depth, cpg, chunks, volume = dims
    per = cpg // chunks
    xs = 2 * size
    xgroups = xs // 8
    everyone = size * depth * 2
    gx, gz, col = lax.axis_index("gx"), lax.axis_index("gz"), lax.axis_index("col")
    me = (gx * depth + gz) * 2 + col
    other = 1 - col
    right, left = lax.rem(gz + 1, depth), lax.rem(gz + depth - 1, depth)
    chan0 = gx * cpg

    def peer(step):
        return lax.rem(gx + step, size)

    def source(step):
        return lax.rem(gx + size - step, size)

    def coords(step):
        index = lax.rem(me + step, everyone)
        return {
            "gx": index // (2 * depth),
            "gz": lax.rem(index // 2, depth),
            "col": lax.rem(index, 2),
        }

    barrier = pltpu.get_barrier_semaphore()

    @pl.loop(1, everyone)
    def _(step):
        pl.semaphore_signal(barrier, inc=1, device_id=coords(step), device_id_type=MESH)

    pl.semaphore_wait(barrier, everyone - 1)

    def remote(src, dst, send, rec, device):
        return pltpu.make_async_remote_copy(
            src_ref=src, dst_ref=dst, send_sem=send, recv_sem=rec,
            device_id=device, device_id_type=MESH,
        )

    def a_copy(chunk, step):
        return remote(
            feat.at[pl.ds(peer(step) * cpg + chunk * per, per)],
            recv.at[step, pl.ds(chunk * per, per)],
            a_send.at[chunk, step], a_recv.at[chunk, step], {"gx": peer(step)},
        )

    def h_copy(way, step):
        return remote(
            halo_out.at[peer(step)], halo_in.at[way, step],
            h_send.at[way, step], h_recv.at[way, step],
            {"gx": peer(step), "gz": right if way == 0 else left},
        )

    own_copy = pltpu.make_async_copy(feat.at[pl.ds(chan0, cpg)], recv.at[0], own_sem)
    own_copy.start()
    for step in range(1, size):
        a_copy(0, step).start()

    lane = lax.broadcasted_iota(jnp.int32, (8, 128), 1)
    quad = lane // 4

    @pl.loop(0, size)
    def _(group):
        for first in range(0, cpg, 4):
            packed = jnp.zeros((8, 128), F32)
            for c in range(first, min(first + 4, cpg)):
                stage[c] = feat[group * cpg + c].astype(F32)
                for xl in range(2):
                    rows = stage[c, pl.ds(xl, 32, stride=2), :]
                    for t in range(4):
                        m = (c - first) * 8 + xl * 4 + t
                        turned = pltpu.roll(rows[8 * t : 8 * t + 8], (2 + 4 * m) % 128, 1)
                        packed = jnp.where(quad == m, turned, packed)
            halo_out[group, pl.ds(first // 4 * 8, 8), :] = packed

    for way in range(2):
        for step in range(size):
            h_copy(way, step).start()
    for chunk in range(1, chunks):
        for step in range(1, size):
            a_copy(chunk, step).start()

    band_pad[0:8] = jnp.zeros((8, 9), F32)
    band_pad[8:72] = bands[...]
    band_pad[72:80] = jnp.zeros((8, 9), F32)
    for k in range(9):
        band_rows[k] = jnp.broadcast_to(band_pad[pl.ds(32 * col, 48), k : k + 1], (48, 128))

    @pl.loop(0, cpg)
    def _(c):
        for k in range(9):
            taps[c, k] = wall_w[k, chan0 + c] * band_rows[k]
        for x_group in range(0, xs, 8):
            blank = jnp.zeros((8, 8, 128), F32)
            smooth[c, pl.ds(x_group, 8), pl.ds(pl.multiple_of(40 * col, 8), 8), :] = blank
            gwall[c, pl.ds(x_group, 8), pl.ds(pl.multiple_of(40 * col, 8), 8), :] = blank
        for q in range(40):
            acc[c, q] = jnp.zeros((8, 128), F32)

    red[...] = jnp.zeros((128, 128), F32)

    def shifts(value, edge):
        return (
            pltpu.roll(jnp.where(lane >= 126, edge, value), 2, 1),
            pltpu.roll(jnp.where(lane == 127, edge, value), 1, 1),
            value,
            pltpu.roll(jnp.where(lane == 0, edge, value), 127, 1),
            pltpu.roll(jnp.where(lane < 2, edge, value), 126, 1),
        )

    def filtered(field, c, x, flip):
        total = None
        for i in range(5):
            at = lax.rem(x + (4 - i if flip else i) - 2 + xs, xs)
            for j in range(5):
                term = tile_w[chan0 + c, 5 * i + j] * field[4 - j if flip else j, c, at]
                total = term if total is None else total + term
        return total

    def y_copy(ref, index, send, rec):
        src = pl.multiple_of(32 - 24 * col, 8)
        dst = pl.multiple_of(40 * col, 8)
        return remote(
            ref.at[index + (pl.ds(src, 8),)], ref.at[index + (pl.ds(dst, 8),)],
            send, rec, {"col": other},
        )

    def s_copy(c):
        return y_copy(smooth, (c, pl.ds(0, xs)), s_send.at[c], s_recv.at[c])

    own_copy.wait()
    for way in range(2):
        for step in range(size):
            h_copy(way, step).wait_recv()

    def edges_of(ref_left, ref_right):
        return jnp.where(lax.rem(lane, 4) < 2, ref_left, ref_right)

    for chunk in range(chunks):
        for step in range(1, size):
            a_copy(chunk, step).wait_recv()
        for c in range(chunk * per, chunk * per + per):

            @pl.loop(0, size, unroll=2)
            def _(step, c=c):
                s = source(step)
                stage[step] = recv[step, c].astype(F32)
                at = pl.ds(c // 4 * 8, 8)
                packed = edges_of(halo_in[0, step, at, :], halo_in[1, step, at, :])
                for xl in range(2):
                    rows = stage[step, pl.ds(xl, 32, stride=2), :]
                    for t in range(4):
                        m = c % 4 * 8 + xl * 4 + t
                        edge = pltpu.roll(packed, (126 - 4 * m) % 128, 1)
                        moved = shifts(rows[8 * t : 8 * t + 8], edge)
                        for j in range(5):
                            zfeat[j, c, 2 * s + xl, pl.ds(8 * t, 8), :] = moved[j]

            @pl.loop(0, xs, unroll=4)
            def _(x, c=c):
                smooth[c, x, pl.ds(8, 32), :] = rounded(filtered(zfeat, c, x, False))

            s_copy(c).start()

    for c in range(cpg):
        s_copy(c).wait_recv()

    def p_copy(step):
        return remote(
            part_out.at[step], part_in.at[step], p_send.at[step], p_recv.at[step],
            {"gx": peer(step)},
        )

    def scores_at(x):
        def body(c, totals):
            wall = None
            for k in range(9):
                term = taps[c, k, pl.ds(8, 32), :] * smooth[c, x, pl.ds(4 + k, 32), :]
                wall = term if wall is None else wall + term
            sig = jax.nn.sigmoid(wall)
            hidden = wall * sig
            hid[c, x] = hidden
            slope[c, x] = sig * (1.0 + wall * (1.0 - sig))
            return tuple(
                total + class_w[k, chan0 + c] * hidden for k, total in enumerate(totals)
            )

        return lax.fori_loop(
            0, cpg, body, tuple(jnp.zeros((32, 128), F32) for k in range(4)), unroll=min(4, cpg)
        )

    @pl.loop(1, size)
    def _(step):
        for xl in range(2):
            totals = scores_at(2 * peer(step) + xl)
            for k in range(4):
                part_out[step, pl.ds((2 * k + xl) * 32, 32), :] = totals[k].astype(BF16)
        p_copy(step).start()

    for xl in range(2):
        totals = scores_at(2 * gx + xl)
        for k in range(4):
            part_own[pl.ds((2 * k + xl) * 32, 32), :] = totals[k]

    @pl.loop(1, size)
    def _(step):
        p_copy(step).wait_recv()
        part_own[...] = part_own[...] + part_in[step].astype(F32)

    for xl in range(2):
        marks = labels[pl.ds(64 * col + xl, 32, stride=2), :]
        for k in range(4):
            at = pl.ds((2 * k + xl) * 32, 32)
            err[0, at, :] = (part_own[at, :] - jnp.where(marks == k, 1.0, 0.0)).astype(BF16)

    def e_copy(step):
        return remote(
            err.at[0], err.at[step], e_send.at[step], e_recv.at[step], {"gx": peer(step)}
        )

    for step in range(1, size):
        e_copy(step).start()

    def w_copy(step):
        return y_copy(
            gwall, (pl.ds(0, cpg), pl.ds(2 * source(step), 2)), w_send.at[step], w_recv.at[step]
        )

    def wall_grads(step):
        for xl in range(2):
            x = 2 * source(step) + xl
            errors = [err[step, pl.ds((2 * k + xl) * 32, 32), :].astype(F32) for k in range(4)]

            @pl.loop(0, cpg, unroll=min(4, cpg))
            def _(c):
                hidden = hid[c, x]
                grad = None
                for k in range(4):
                    term = class_w[k, chan0 + c] * errors[k]
                    grad = term if grad is None else grad + term
                    acc[c, 34 + k] = acc[c, 34 + k] + fold(errors[k] * hidden)
                gwall[c, x, pl.ds(8, 32), :] = rounded(grad * slope[c, x])

        w_copy(step).start()

    wall_grads(0)

    @pl.loop(1, size)
    def _(step):
        e_copy(step).wait_recv()
        wall_grads(step)

    @pl.loop(0, size)
    def _(step):
        w_copy(step).wait_recv()

    def g_copy(way, c):
        return remote(
            ghalo_out.at[c], ghalo_in.at[way, c], g_send.at[way, c], g_recv.at[way, c],
            {"gz": right if way == 0 else left},
        )

    @pl.loop(0, cpg)
    def _(c):
        def body(x, sums9):
            grad = gwall[c, x, pl.ds(8, 32), :]
            total = None
            news = []
            for k in range(9):
                term = taps[c, k, pl.ds(12 - k, 32), :] * gwall[c, x, pl.ds(12 - k, 32), :]
                total = term if total is None else total + term
                product = grad * band_rows[k, pl.ds(8, 32), :] * smooth[c, x, pl.ds(4 + k, 32), :]
                news.append(sums9[k] + fold(product))
            gsm[c, x] = rounded(total)
            return tuple(news)

        sums9 = lax.fori_loop(0, xs, body, tuple(jnp.zeros((8, 128), F32) for k in range(9)), unroll=2)
        for k in range(9):
            acc[c, 25 + k] = sums9[k]

        @pl.loop(0, xgroups)
        def _(group):
            packed = jnp.zeros((8, 128), F32)
            for m in range(32):
                piece = gsm[c, group * 8 + m // 4, pl.ds(m % 4 * 8, 8), :]
                packed = jnp.where(quad == m, pltpu.roll(piece, (2 + 4 * m) % 128, 1), packed)
            ghalo_out[c, group] = packed

        for way in range(2):
            g_copy(way, c).start()

    def o_copy(chunk, step):
        return remote(
            gout.at[peer(step), pl.ds(chunk * per, per)],
            out.at[pl.ds(chan0 + chunk * per, per)],
            o_send.at[chunk, step], o_recv.at[chunk, step], {"gx": peer(step)},
        )

    @pl.loop(0, chunks)
    def _(chunk):
        @pl.loop(0, per)
        def _(lower):
            c = chunk * per + lower
            for way in range(2):
                g_copy(way, c).wait_recv()

            @pl.loop(0, xgroups)
            def _(group):
                packed = edges_of(ghalo_in[0, c, group], ghalo_in[1, c, group])
                for m in range(32):
                    at = pl.ds(m % 4 * 8, 8)
                    x = group * 8 + m // 4
                    edge = pltpu.roll(packed, (126 - 4 * m) % 128, 1)
                    moved = shifts(gsm[c, x, at, :], edge)
                    for j in range(5):
                        zgrad[j, c, x, at, :] = moved[j]

            @pl.loop(0, size, unroll=2)
            def _(s):
                for xl in range(2):
                    gstage[s, pl.ds(xl, 32, stride=2), :] = filtered(zgrad, c, 2 * s + xl, True)
                gout[s, c] = gstage[s].astype(BF16)

            out[chan0 + c] = gout[gx, c]

        for step in range(1, size):
            o_copy(chunk, step).start()

    row = lax.broadcasted_iota(jnp.int32, (8, 128), 0)

    @pl.loop(0, cpg)
    def _(c):
        def body(x, sums25):
            grad = gsm[c, x]
            news = []
            for i in range(5):
                at = lax.rem(x + i - 2 + xs, xs)
                for j in range(5):
                    news.append(sums25[5 * i + j] + fold(zfeat[j, c, at] * grad))
            return tuple(news)

        sums25 = lax.fori_loop(0, xs, body, tuple(jnp.zeros((8, 128), F32) for q in range(25)), unroll=2)
        for q in range(38):
            value = sums25[q] if q < 25 else acc[c, q]
            red[pl.ds(q, 1), :] = jnp.sum(value, axis=0, keepdims=True)
        line = lax.dot_general(
            jnp.ones((8, 128), F32), red[...], (((1,), (1,)), ((), ())),
            precision=lax.Precision.HIGHEST, preferred_element_type=F32,
        )
        before = jnp.where(c == 0, jnp.zeros((8, 128), F32), sums[me])
        sums[me] = jnp.where(row == c, line, before)

    def r_copy(step):
        return remote(sums.at[me], sums.at[me], r_send.at[step], r_recv.at[step], coords(step))

    @pl.loop(1, everyone)
    def _(step):
        r_copy(step).start()

    @pl.loop(1, everyone)
    def _(step):
        r_copy(step).wait_recv()

    @pl.loop(0, size)
    def _(group):
        total = sums[group * depth * 2]
        for member in range(1, depth * 2):
            total = total + sums[group * depth * 2 + member]
        red[pl.ds(group * cpg, cpg), :] = total[0:cpg] / volume

    turned = red[...].T
    chans = size * cpg
    tile_out[...] = red[0:chans, 0:25]
    wall_out[...] = turned[25:34, 0:chans]
    class_out[...] = turned[34:38, 0:chans]

    for chunk in range(chunks):
        for step in range(1, size):
            o_copy(chunk, step).wait()
            a_copy(chunk, step).wait_send()
    for way in range(2):
        for step in range(size):
            h_copy(way, step).wait_send()
        for c in range(cpg):
            g_copy(way, c).wait_send()
    for c in range(cpg):
        s_copy(c).wait_send()
    for step in range(1, size):
        p_copy(step).wait_send()
        e_copy(step).wait_send()
    for step in range(size):
        w_copy(step).wait_send()

    @pl.loop(1, everyone)
    def _(step):
        r_copy(step).wait_send()


def shards(features, labels, grid_index, stretch, tile_filter, wall_filter, class_weight):
    chans, rows, cells_x, cells_z = features.shape
    size, depth = lax.axis_size("gx"), lax.axis_size("gz")
    volume = labels.shape[0] * cells_x * size * cells_z * depth
    cpg = chans // size
    chunks = min(4, cpg)
    per_dest = max(cpg // 4, 1) * 8
    xs = 2 * size
    everyone = size * depth * 2
    onehot = (grid_index[:, None] == jnp.arange(stretch.shape[0], dtype=jnp.int32)).astype(F32)
    bands = jnp.dot(onehot, stretch, precision=lax.Precision.HIGHEST)
    dma = pltpu.SemaphoreType.DMA
    vmem = pl.BlockSpec(memory_space=pltpu.VMEM)
    smem = pl.BlockSpec(memory_space=pltpu.SMEM)
    grad, tile_grad, wall_grad, class_grad = pl.pallas_call(
        functools.partial(kernel, (size, depth, cpg, chunks, volume)),
        out_shape=(
            jax.ShapeDtypeStruct((chans, 64, 128), BF16),
            jax.ShapeDtypeStruct((chans, 25), F32),
            jax.ShapeDtypeStruct((9, chans), F32),
            jax.ShapeDtypeStruct((4, chans), F32),
        ),
        in_specs=[vmem, vmem, vmem, smem, smem, smem],
        out_specs=(vmem, vmem, vmem, vmem),
        scratch_shapes=[
            pltpu.VMEM((size, cpg, 64, 128), BF16),
            pltpu.VMEM((80, 9), F32),
            pltpu.VMEM((size, per_dest, 128), F32),
            pltpu.VMEM((2, size, per_dest, 128), F32),
            pltpu.VMEM((5, cpg, xs, 32, 128), F32),
            pltpu.VMEM((cpg, xs, 48, 128), F32),
            pltpu.VMEM((max(cpg, size), 64, 128), F32),
            pltpu.VMEM((cpg, 9, 48, 128), F32),
            pltpu.VMEM((9, 48, 128), F32),
            pltpu.VMEM((cpg, xs, 32, 128), F32),
            pltpu.VMEM((cpg, xs, 32, 128), F32),
            pltpu.VMEM((256, 128), F32),
            pltpu.VMEM((size, 256, 128), BF16),
            pltpu.VMEM((size, 256, 128), BF16),
            pltpu.VMEM((size, 256, 128), BF16),
            pltpu.VMEM((cpg, xs, 48, 128), F32),
            pltpu.VMEM((cpg, xs, 32, 128), F32),
            pltpu.VMEM((cpg, xs // 8, 8, 128), F32),
            pltpu.VMEM((2, cpg, xs // 8, 8, 128), F32),
            pltpu.VMEM((5, cpg, xs, 32, 128), F32),
            pltpu.VMEM((size, cpg, 64, 128), BF16),
            pltpu.VMEM((size, 64, 128), F32),
            pltpu.VMEM((cpg, 40, 8, 128), F32),
            pltpu.VMEM((128, 128), F32),
            pltpu.VMEM((everyone, 8, 128), F32),
            dma((chunks, size)), dma((chunks, size)), dma(()),
            dma((2, size)), dma((2, size)),
            dma((cpg,)), dma((cpg,)),
            dma((size,)), dma((size,)),
            dma((size,)), dma((size,)),
            dma((size,)), dma((size,)),
            dma((2, cpg)), dma((2, cpg)),
            dma((chunks, size)), dma((chunks, size)),
            dma((everyone,)), dma((everyone,)),
        ],
        compiler_params=pltpu.CompilerParams(
            collective_id=0, has_side_effects=True, vmem_limit_bytes=48 * 1024 * 1024
        ),
    )(
        features.reshape(chans, 64, 128), labels.reshape(128, 128), bands,
        tile_filter, wall_filter.T, class_weight,
    )
    return grad.reshape(features.shape), tile_grad, wall_grad.T, class_grad


def solution(mesh):
    return jax.shard_map(
        shards,
        mesh=mesh,
        in_specs=(
            P(None, "col", ("group", "gx"), "gz"),
            P(None, ("group", "gx"), "gz"),
            P(),
            P(),
            P(),
            P(),
            P(),
        ),
        out_specs=(
            P(None, "col", ("group", "gx"), "gz"),
            P("group", None),
            P("group", None),
            P("group", None),
        ),
        check_vma=False,
    )
```

profile of v0, /device:TPU:0, one launch (start us, length us, event | category | flops | bytes accessed | tf_op | source)
XLA Modules:
  0.0 68.4 jit_solution(2412130585921756764)
XLA Ops:
  0.6 0.0 copy-start
  0.6 0.0 copy-start.2
  0.7 0.7 copy-done
  1.3 0.0 copy-start.5
  1.3 0.9 %fusion.bands = f32[64,9]{1,0:T(8,128)S(1)} fusion(f32[16,9]{1,0:T(8,128)S(1)} %copy-done, s32[64]{0:T(128)} %param.9), kind=kOutput, calls=%fused_computation.1 | convolution fusion | flops 111616 | bytes 3136 | tf_op jit(solution)/shard_map/dot_general | solution.py:444
  2.2 0.0 copy-done.2
  2.2 0.0 copy-done.5
  2.2 0.0 copy-start.1
  2.2 1.0 %copy-done.1 = bf16[32,32,2,128]{3,2,1,0:T(2,128)(2,1)S(1)} copy-done((bf16[32,32,2,128]{3,2,1,0:T(2,128)(2,1)S(1)}, bf16[32,32,2,128]{3,2,1,0:T(2,128)(2,1)}, u32[]{:S(2)}) %copy-start.1) | copy-done | bytes 524312
  3.3 0.0 copy-start.3
  3.3 0.7 %copy-done.3 = f32[32,25]{1,0:T(8,128)S(1)} copy-done((f32[32,25]{1,0:T(8,128)S(1)}, f32[32,25]{1,0:T(8,128)}, u32[]{:S(2)}) %copy-start.3) | copy-done | bytes 3224
  4.0 0.0 copy-start.4
  4.0 0.7 %copy-done.4 = f32[32,9]{0,1:T(8,128)S(1)} copy-done((f32[32,9]{0,1:T(8,128)S(1)}, f32[32,9]{0,1:T(8,128)}, u32[]{:S(2)}) %copy-start.4) | copy-done | bytes 1176
  4.7 61.2 %shard_map.102 = (bf16[32,64,128]{2,1,0:T(8,128)(2,1)S(1)}, f32[32,25]{1,0:T(8,128)S(1)}, f32[9,32]{1,0:T(8,128)S(1)}, f32[4,32]{1,0:T(4,128)S(1)}) custom-call(bf16[32,64,128]{2,1,0:T(8,128)(2,1)S(1)} %bitcast.6, s32[128,128]{1,0:T(8,128)S(1)} %bitcast.8, f32[64,9]{1,0:T(8,128)S(1)} %fusion.bands, f32[32,25]{1,0:T(8,128)S(1)} %copy-done.3, ...), custom_call_target="tpu_custom_call" | custom-call | tf_op jit(solution)/shard_map/pallas_call | solution.py:448
  65.9 0.8 %copy.17 = bf16[32,32,2,128]{3,2,1,0:T(2,128)(2,1)} copy(bf16[32,32,2,128]{3,2,1,0:T(2,128)(2,1)S(1)} %bitcast.7) | data formatting | bytes 1048576
  66.7 0.6 copy.18
  67.3 0.6 copy.19
  67.9 0.6 copy.20
Async XLA Ops:
  0.6 0.7 %copy-start = (f32[16,9]{1,0:T(8,128)S(1)}, f32[16,9]{1,0:T(8,128)}, u32[]{:S(2)}) copy-start(f32[16,9]{1,0:T(8,128)} %param.10) | copy-start | bytes 1732
  0.6 1.6 %copy-start.2 = (s32[64,2,128]{2,1,0:T(2,128)S(1)}, s32[64,2,128]{2,1,0:T(2,128)}, u32[]{:S(2)}) copy-start(s32[64,2,128]{2,1,0:T(2,128)} %param.8) | copy-start | bytes 196612
  1.3 0.9 %copy-start.5 = (f32[4,32]{1,0:T(4,128)S(1)}, f32[4,32]{1,0:T(4,128)}, u32[]{:S(2)}) copy-start(f32[4,32]{1,0:T(4,128)} %class_w.1) | copy-start | bytes 1540
  2.2 1.0 %copy-start.1 = (bf16[32,32,2,128]{3,2,1,0:T(2,128)(2,1)S(1)}, bf16[32,32,2,128]{3,2,1,0:T(2,128)(2,1)}, u32[]{:S(2)}) copy-start(bf16[32,32,2,128]{3,2,1,0:T(2,128)(2,1)} %param.7) | copy-start | bytes 1572868
  3.3 0.7 %copy-start.3 = (f32[32,25]{1,0:T(8,128)S(1)}, f32[32,25]{1,0:T(8,128)}, u32[]{:S(2)}) copy-start(f32[32,25]{1,0:T(8,128)} %tile_w.1) | copy-start | bytes 9604
  4.0 0.7 %copy-start.4 = (f32[32,9]{0,1:T(8,128)S(1)}, f32[32,9]{0,1:T(8,128)}, u32[]{:S(2)}) copy-start(f32[32,9]{0,1:T(8,128)} %param.12) | copy-start | bytes 3460
where the time goes:
time: 68.8 us; the launch traced here: 68.4 us
  Pallas kernels  61.2 us (89%)
  local copies, waits for them, and re-layouts  5.72 us (8%)
  matrix products  0.87 us (1%)
  between operations  0.69 us (1%)
    pallas_call x1, Pallas kernels, shards(): pl.pallas_call(functools.partial(kernel, (size, depth, cpg, chunks, volum...  61.2 us
    unnamed x16, local copies, waits for them, and re-layouts  5.72 us

commit v1 on v0

--- a/solution.py
+++ b/solution.py
@@ -431,11 +431,699 @@
         r_copy(step).wait_send()
 
 
+OWN = 32
+WIN = OWN + 8
+BLOCK = 12
+BLOCKS = (WIN - 4) // BLOCK
+ROWS = BLOCK * 8
+HALF = ROWS // 2
+PIECES = ((0, 2), (2, 6), (8, 6), (14, 4), (18, 2))
+ARRIVE = ((0, 1), (2,), (3, 4))
+WANTED = 38
+HIGH = lax.Precision.HIGHEST
+
+
+def dot(a, b, dims=((1,), (0,))):
+    return lax.dot_general(a, b, (dims, ((), ())), precision=HIGH, preferred_element_type=F32)
+
+
+def region_kernel(
+    dims,
+    feat_h, lab_h, index_h, stretch_h, tile_h, wall_h, class_h,
+    out, tile_out, wall_out, class_out,
+    feat, lab, index, stretch, tile_w, wall_w, class_w,
+    turn, send, recv, lab_rows, lab_send, lab_recv, lab_wide, lab_win,
+    field, odd, smooth, gwall, gsm, godd, hid, slope, part_out, part_in,
+    taps, fore, back, band_back, wall_acc, acc, gram, params, classes, classes_t,
+    gout, ghome, sums, red,
+    in_sem, f_send, f_recv, l_send, l_recv, p_send, p_recv, g_send, g_recv, r_send, r_recv,
+):
+    size, depth, volume = dims
+    everyone = size * depth * 2
+    gx, gz, col = lax.axis_index("gx"), lax.axis_index("gz"), lax.axis_index("col")
+    me = (gx * depth + gz) * 2 + col
+    right, left = lax.rem(gz + 1, depth), lax.rem(gz + depth - 1, depth)
+    zps = OWN // 2
+    lane = lax.broadcasted_iota(jnp.int32, (8, 128), 1)
+    row = lax.broadcasted_iota(jnp.int32, (8, 128), 0)
+    first = lane < 64
+    y_lane = lax.rem(lane, 64) // 2
+    x_even = lax.rem(lane, 2) == 0
+
+    ins = [
+        pltpu.make_async_copy(src, dst, in_sem.at[n])
+        for n, (src, dst) in enumerate((
+            (feat_h, feat), (lab_h, lab), (index_h, index), (stretch_h, stretch),
+            (tile_h, tile_w), (wall_h, wall_w), (class_h, class_w),
+        ))
+    ]
+    for copy in ins:
+        copy.start()
+
+    def coords(step):
+        place = lax.rem(me + step, everyone)
+        return {
+            "gx": place // (2 * depth),
+            "gz": lax.rem(place // 2, depth),
+            "col": lax.rem(place, 2),
+        }
+
+    barrier = pltpu.get_barrier_semaphore()
+
+    @pl.loop(1, everyone)
+    def _(step):
+        pl.semaphore_signal(barrier, inc=1, device_id=coords(step), device_id_type=MESH)
+
+    def remote(src, dst, sent, got, device):
+        return pltpu.make_async_remote_copy(
+            src_ref=src, dst_ref=dst, send_sem=sent, recv_sem=got,
+            device_id=device, device_id_type=MESH,
+        )
+
+    def target(sx):
+        return lax.rem(gx + sx, size)
+
+    def origin(sx):
+        return lax.rem(gx + size - sx, size)
+
+    ins[0].wait()
+    for side in range(2):
+        for cp in range(8):
+            block = feat[pl.ds(side * 16 + 2 * cp, 2)].astype(F32).reshape(128, 128)
+            turn[side, pl.ds(cp, 128, stride=8), :] = block.T
+
+        @pl.loop(0, 64, unroll=8)
+        def _(zp, side=side):
+            at = pl.ds(pl.multiple_of(zp * 16, 16), 16)
+            send[side, zp] = turn[side, at, :].astype(BF16)
+
+    ins[1].wait()
+    turn[2, 0:128, :] = lab[...].astype(F32).T
+    even, uneven = turn[2, pl.ds(0, 64, stride=2), :], turn[2, pl.ds(1, 64, stride=2), :]
+    here = jnp.where(col == 0, even, pltpu.roll(even, 64, 1))
+    there = jnp.where(col == 0, pltpu.roll(uneven, 64, 1), uneven)
+    lab_rows[...] = jnp.where(lax.broadcasted_iota(jnp.int32, (64, 128), 1) < 64, here, there)
+    for t in range(size):
+        lab_send[t] = lab_rows[pl.ds(zps * t, zps), :].astype(BF16)
+    edge_rows = [jnp.zeros((1, 128), F32)] * 16
+    for t in range(size):
+        edge_rows[2 * t] = lab_rows[pl.ds((zps * t - 1) % 64, 1), :]
+        edge_rows[2 * t + 1] = lab_rows[pl.ds((zps * t + zps) % 64, 1), :]
+    lab_send[size] = jnp.concatenate(edge_rows, axis=0).astype(BF16)
+
+    pl.semaphore_wait(barrier, everyone - 1)
+
+    def f_spot(piece, t):
+        at, count = PIECES[piece]
+        return pl.ds(lax.rem(t * zps + at - 2 + 64, 64), count), pl.ds(at, count)
+
+    def f_far(piece, sx, sc):
+        t, ct = target(sx), lax.rem(col + sc, 2)
+        src, dst = f_spot(piece, t)
+        if piece == 0:
+            tz = lax.rem(gz + 1 - (t + size - 1) // size, depth)
+        elif piece == len(PIECES) - 1:
+            tz = lax.rem(gz + depth - (t + 1) // size, depth)
+        else:
+            tz = gz
+        return remote(
+            send.at[ct, src], recv.at[gx, col, dst],
+            f_send.at[piece, sx, sc], f_recv.at[piece, sx, sc],
+            {"gx": t, "gz": tz, "col": ct},
+        )
+
+    def f_near(piece):
+        src, dst = f_spot(piece, gx)
+        return pltpu.make_async_copy(
+            send.at[col, src], recv.at[gx, col, dst], f_recv.at[piece, 0, 0]
+        )
+
+    def f_wait(piece, sx, sc):
+        at, count = PIECES[piece]
+        slot = recv.at[origin(sx), lax.rem(col + sc, 2), pl.ds(at, count)]
+        return remote(
+            slot, slot, f_send.at[piece, sx, sc], f_recv.at[piece, sx, sc],
+            {"gx": target(sx), "gz": gz, "col": lax.rem(col + sc, 2)},
+        )
+
+    def own_piece(piece, near, far):
+        if piece == 0:
+            pl.when(gx > 0)(near)
+            pl.when(gx == 0)(far)
+        elif piece == len(PIECES) - 1:
+            pl.when(gx < size - 1)(near)
+            pl.when(gx == size - 1)(far)
+        else:
+            near()
+
+    others = [(sx, sc) for sx in (2, 1, 3, 0) for sc in range(2) if sx or sc]
+
+    def l_mid(sx):
+        return remote(
+            lab_send.at[target(sx)], lab_recv.at[gx, 0], l_send.at[0, sx], l_recv.at[0, sx],
+            {"gx": target(sx)},
+        )
+
+    def l_edge(sx):
+        return remote(
+            lab_send.at[size], lab_recv.at[gx, 1], l_send.at[1, sx], l_recv.at[1, sx],
+            {"gx": target(sx)},
+        )
+
+    def l_far(sx):
+        t = target(sx)
+        tz = lax.rem(gz + depth + 1 - 2 * ((t + 1) // size), depth)
+        return remote(
+            lab_send.at[size], lab_recv.at[gx, 2], l_send.at[2, sx], l_recv.at[2, sx],
+            {"gx": t, "gz": tz},
+        )
+
+    l_own = [
+        pltpu.make_async_copy(lab_send.at[gx], lab_recv.at[gx, 0], l_recv.at[0, 0]),
+        pltpu.make_async_copy(lab_send.at[size], lab_recv.at[gx, 1], l_recv.at[1, 0]),
+    ]
+
+    for block in range(BLOCKS):
+        for piece in ARRIVE[block]:
+            for sx, sc in others:
+                f_far(piece, sx, sc).start()
+            own_piece(
+                piece,
+                lambda piece=piece: f_near(piece).start(),
+                lambda piece=piece: f_far(piece, 0, 0).start(),
+            )
+        if block == 0:
+            for copy in l_own:
+                copy.start()
+            for sx in range(size):
+                if sx:
+                    l_mid(sx).start()
+                    l_edge(sx).start()
+                l_far(sx).start()
+
+    for copy in ins[2:]:
+        copy.wait()
+    params[...] = jnp.zeros((128, 128), F32)
+    params[0:9, 0:32] = wall_w[...]
+    params[16:20, 0:32] = class_w[...]
+    params[64:96, 0:25] = tile_w[...]
+    red[...] = params[...].T
+
+    def pairs(ref, start):
+        return ref[pl.ds(start + col * 16, 8, stride=2), :], ref[pl.ds(start + col * 16 + 1, 8, stride=2), :]
+
+    def spread(both, q):
+        low, high = (jnp.broadcast_to(rows[:, q : q + 1], (8, 128)) for rows in both)
+        return jnp.where(first, low, high)
+
+    tile_pairs, wall_pairs = pairs(params, 64), pairs(red, 0)
+    for q in range(25):
+        taps[q] = spread(tile_pairs, q)
+
+    levels = stretch.shape[0]
+    hot = lax.broadcasted_iota(jnp.int32, (levels, 64), 0) == index[...]
+    params[32:41, 0:64] = dot(stretch[...], hot.astype(F32), ((0,), (0,)))
+    band_t = params[32:48, 0:64]
+    y_row = lax.broadcasted_iota(jnp.int32, (64, 128), 0)
+    y_col = lax.rem(lax.broadcasted_iota(jnp.int32, (64, 128), 1), 64) // 2
+    for yh in range(2):
+        ahead = dot(band_t, (y_row == y_col + 32 * yh).astype(F32))
+        for k in range(9):
+            m = k - 4
+            weight = spread(wall_pairs, k)
+            inside = (y_lane + (32 * yh + m) >= 0) & (y_lane + (32 * yh + m) < 64)
+            fore[k, yh] = jnp.where(inside, weight * ahead[k : k + 1, :], 0.0)
+            behind = dot(band_t, (y_row == y_col + (32 * yh - m)).astype(F32))
+            band_back[k, yh] = jnp.broadcast_to(behind[k : k + 1, :], (8, 128))
+            back[k, yh] = weight * band_back[k, yh]
+            wall_acc[k, yh] = jnp.zeros((8, 128), F32)
+
+    chan = lax.broadcasted_iota(jnp.int32, (128, 128), 0)
+    unit = lax.rem(lax.broadcasted_iota(jnp.int32, (128, 128), 1), 8)
+    half_row = lax.broadcasted_iota(jnp.int32, (HALF, 128), 0)
+    half_z = lax.broadcasted_iota(jnp.int32, (HALF, 128), 1) // 8
+    half_k = lax.rem(half_row, 8) // 2
+    same_z = (half_row // 8) * 2 + lax.rem(half_row, 2) == half_z
+    classes[...] = jnp.zeros((128, 128), F32)
+    for par in range(2):
+        rows = dot(params[16:24, :], (chan == col * 16 + 2 * unit + par).astype(F32))
+        value = jnp.zeros((HALF, 128), F32)
+        for k in range(4):
+            value = jnp.where(same_z & (half_k == k), rows[k : k + 1, :], value)
+        classes[pl.ds(HALF * par, HALF), :] = value
+    classes_t[...] = classes[...].T
+
+    def arrived(block):
+        for piece in ARRIVE[block]:
+            for sx, sc in others:
+                f_wait(piece, sx, sc).wait_recv()
+            own_piece(
+                piece,
+                lambda piece=piece: f_near(piece).wait(),
+                lambda piece=piece: f_wait(piece, 0, 0).wait_recv(),
+            )
+        low, high = PIECES[ARRIVE[block][0]][0], sum(PIECES[ARRIVE[block][-1]])
+
+        @pl.loop(0, 2 * size)
+        def _(t):
+            for zp in range(low, high):
+                pair = recv[t // 2, lax.rem(t, 2), zp].astype(F32)
+                field[t, 2 * zp] = pair[0:8]
+                field[t, 2 * zp + 1] = pair[8:16]
+
+        between(field, odd, 2 * low, 2 * high)
+
+    def between(src, dst, low, high):
+        @pl.loop(0, 2 * size)
+        def _(t):
+            after = lax.rem(t + 2, 2 * size)
+            for z in range(low, high):
+                dst[t, z] = jnp.where(
+                    x_even, pltpu.roll(src[t, z], 127, 1), pltpu.roll(src[after, z], 1, 1)
+                )
+
+    def filtered(src, mid, t, low, count, flip, put):
+        before, after = lax.rem(t + 2 * size - 2, 2 * size), lax.rem(t + 2, 2 * size)
+        totals = [None] * count
+        for z in range(count + 4):
+            at = low + z - 2
+            views = (src[before, at], mid[before, at], src[t, at], mid[t, at], src[after, at])
+            for j in range(5):
+                if 0 <= z - j < count:
+                    for i in range(5):
+                        q = 5 * (4 - i) + 4 - j if flip else 5 * i + j
+                        term = taps[q] * views[i]
+                        old = totals[z - j]
+                        totals[z - j] = term if old is None else old + term
+            if z >= 4:
+                put(z - 4, totals)
+
+    def moved(low, high, low_turned, high_turned, m):
+        if m == 0:
+            return low, high
+        if m > 0:
+            mixed = jnp.where(y_lane < m, high_turned, low)
+            return pltpu.roll(mixed, 128 - 2 * m, 1), pltpu.roll(high, 128 - 2 * m, 1)
+        mixed = jnp.where(y_lane >= 32 + m, low_turned, high)
+        return pltpu.roll(low, -2 * m, 1), pltpu.roll(mixed, -2 * m, 1)
+
+    def p_copy(block):
+        return remote(
+            part_out.at[block], part_in.at[block], p_send.at[block], p_recv.at[block],
+            {"col": 1 - col},
+        )
+
+    def ahead_of(block):
+        base = 2 + BLOCK * block
+
+        @pl.loop(0, 2 * size)
+        def _(t):
+            def put(z, totals):
+                smooth[t, base + z] = rounded(totals[z])
+
+            filtered(field, odd, t, base, BLOCK, False, put)
+
+        @pl.loop(0, BLOCK)
+        def _(z):
+            at = pl.ds(pl.multiple_of(8 * z, 8), 8)
+            for p in range(size):
+                low, high = smooth[2 * p, base + z], smooth[2 * p + 1, base + z]
+                turned = pltpu.roll(low, 64, 1), pltpu.roll(high, 64, 1)
+                walls = [None, None]
+                for k in range(9):
+                    pair = moved(low, high, *turned, k - 4)
+                    for yh in range(2):
+                        term = fore[k, yh] * pair[yh]
+                        walls[yh] = term if walls[yh] is None else walls[yh] + term
+                for yh, wall in enumerate(walls):
+                    sig = jax.nn.sigmoid(wall)
+                    lanes = slice(128 * yh, 128 * yh + 128)
+                    hid[block, p, at, lanes] = wall * sig
+                    slope[block, p, at, lanes] = sig * (1.0 + wall * (1.0 - sig))
+
+        left_half = lax.rem(lax.broadcasted_iota(jnp.int32, (HALF, 256), 1), 128) < 64
+
+        @pl.loop(0, size)
+        def _(p):
+            part = dot(classes[0:ROWS, 0:ROWS], hid[block, p])
+            part_out[block, p] = jnp.where(left_half, part[0:HALF], part[HALF:ROWS])
+            lanes = pl.ds(pl.multiple_of(128 * col, 128), 128)
+            for zp in range(BLOCK // 2):
+                at = slice(8 * zp, 8 * zp + 8)
+                mark = lab_win[p, pl.ds(BLOCK // 2 * block + zp, 1), :]
+                mark = jnp.broadcast_to(mark, (8, 128))
+                mark = jnp.where(lax.rem(row, 2) == 0, mark, pltpu.roll(mark, 64, 1))
+                hit = first & (mark == (row // 2).astype(F32))
+                part_out[block, p, at, lanes] = part_out[block, p, at, lanes] - jnp.where(hit, 1.0, 0.0)
+
+        p_copy(block).start()
+
+    def back_of(block):
+        base = 2 + BLOCK * block
+        p_copy(block).wait_recv()
+        left_half = lax.rem(lax.broadcasted_iota(jnp.int32, (HALF, 256), 1), 128) < 64
+
+        @pl.loop(0, size)
+        def _(p):
+            err = part_out[block, p] + part_in[block, p]
+            swapped = jnp.concatenate(
+                [pltpu.roll(err[:, 0:128], 64, 1), pltpu.roll(err[:, 128:256], 64, 1)], axis=1
+            )
+            err = err + swapped
+            both = jnp.concatenate(
+                [jnp.where(left_half, err, 0.0), jnp.where(left_half, 0.0, err)], axis=0
+            )
+            grad = dot(classes_t[0:ROWS, 0:ROWS], both) * slope[block, p]
+            for z in range(BLOCK):
+                for yh in range(2):
+                    gwall[2 * p + yh, base + z] = rounded(
+                        grad[8 * z : 8 * z + 8, 128 * yh : 128 * yh + 128]
+                    )
+            new = dot(both, hid[block, p], ((1,), (1,)))
+            gram[block, p] = new
+
+        @pl.loop(0, BLOCK)
+        def _(z):
+            own = (base + z >= 4) & (base + z < 4 + OWN)
+            sums9 = [[None, None] for k in range(9)]
+            for p in range(size):
+                low, high = gwall[2 * p, base + z], gwall[2 * p + 1, base + z]
+                turned = pltpu.roll(low, 64, 1), pltpu.roll(high, 64, 1)
+                fields = [
+                    jnp.where(own, smooth[2 * p + yh, base + z], 0.0) for yh in range(2)
+                ]
+                totals = [None, None]
+                for k in range(9):
+                    pair = moved(low, high, *turned, 4 - k)
+                    for yh in range(2):
+                        term = back[k, yh] * pair[yh]
+                        totals[yh] = term if totals[yh] is None else totals[yh] + term
+                        term = pair[yh] * fields[yh]
+                        old = sums9[k][yh]
+                        sums9[k][yh] = term if old is None else old + term
+                for yh in range(2):
+                    gsm[2 * p + yh, base + z] = rounded(totals[yh])
+            for k in range(9):
+                for yh in range(2):
+                    wall_acc[k, yh] = wall_acc[k, yh] + sums9[k][yh]
+
+        between(gsm, godd, base, base + BLOCK)
+
+    def g_spot(block):
+        low = 4 if block == 0 else BLOCK * block
+        return low, BLOCK * block + BLOCK - low
+
+    def g_copy(block, step):
+        low, count = g_spot(block)
+        at, many = (low - 4) // 2, count // 2
+        p, yh = target(step // 2), lax.rem(col + step, 2)
+        return remote(
+            gout.at[2 * p + yh, pl.ds(at, many)],
+            ghome.at[col, pl.ds(gx * zps + at, many)],
+            g_send.at[block, step], g_recv.at[block, step], {"gx": p, "col": yh},
+        )
+
+    def g_near(block):
+        low, count = g_spot(block)
+        at, many = (low - 4) // 2, count // 2
+        return pltpu.make_async_copy(
+            gout.at[2 * gx + col, pl.ds(at, many)],
+            ghome.at[col, pl.ds(gx * zps + at, many)],
+            g_recv.at[block, 0],
+        )
+
+    def g_wait(block, step):
+        low, count = g_spot(block)
+        at, many = (low - 4) // 2, count // 2
+        slot = ghome.at[lax.rem(col + step, 2), pl.ds(origin(step // 2) * zps + at, many)]
+        return remote(
+            slot, slot, g_send.at[block, step], g_recv.at[block, step],
+            {"gx": target(step // 2), "col": lax.rem(col + step, 2)},
+        )
+
+    def home(block):
+        low, count = g_spot(block)
+
+        @pl.loop(0, 2 * size)
+        def _(turn_at):
+            step = lax.rem(turn_at + 4, 2 * size)
+            t = 2 * target(step // 2) + lax.rem(col + step, 2)
+
+            def put(z, totals):
+                if z % 2:
+                    pair = jnp.concatenate([totals[z - 1], totals[z]], axis=0)
+                    gout[t, (low - 4 + z) // 2] = pair.astype(BF16)
+
+            filtered(gsm, godd, t, low, count, True, put)
+
+            @pl.when(step > 0)
+            def _():
+                g_copy(block, step).start()
+
+            @pl.when(step == 0)
+            def _():
+                g_near(block).start()
+
+    def labels_in():
+        for sx in range(size):
+            if sx:
+                for slot in range(2):
+                    at = lab_recv.at[origin(sx), slot]
+                    remote(
+                        at, at, l_send.at[slot, sx], l_recv.at[slot, sx], {"gx": target(sx)}
+                    ).wait_recv()
+            at = lab_recv.at[origin(sx), 2]
+            remote(
+                at, at, l_send.at[2, sx], l_recv.at[2, sx], {"gx": target(sx), "gz": right}
+            ).wait_recv()
+        for copy in l_own:
+            copy.wait()
+        low_edge = 2 - (gx + size - 1) // size
+        high_edge = 1 + (gx + 1) // size
+        for p in range(size):
+            lab_win[p, 1 : 1 + zps, :] = lab_recv[p, 0].astype(F32)
+            for slot in range(1, 3):
+                lab_wide[p, slot] = lab_recv[p, slot].astype(F32)
+            lab_win[p, 0:1, :] = lab_wide[p, low_edge, pl.ds(2 * gx, 1), :]
+            lab_win[p, 1 + zps : 2 + zps, :] = lab_wide[p, high_edge, pl.ds(2 * gx + 1, 1), :]
+
+    arrived(0)
+    labels_in()
+    ahead_of(0)
+    arrived(1)
+    ahead_of(1)
+    back_of(0)
+    home(0)
+    arrived(2)
+    ahead_of(2)
+    back_of(1)
+    home(1)
+    back_of(2)
+    home(2)
+
+    def tile_body(it, sums25):
+        t, base = it // 4, 4 + 8 * lax.rem(it, 4)
+        before, after = lax.rem(t + 2 * size - 2, 2 * size), lax.rem(t + 2, 2 * size)
+        grads = [gsm[t, base + z] for z in range(8)]
+        news = list(sums25)
+        for z in range(12):
+            at = base + z - 2
+            views = (
+                field[before, at], odd[before, at], field[t, at], odd[t, at], field[after, at]
+            )
+            for j in range(5):
+                if 0 <= z - j < 8:
+                    for i in range(5):
+                        news[5 * i + j] = news[5 * i + j] + views[i] * grads[z - j]
+        return tuple(news)
+
+    sums25 = lax.fori_loop(
+        0, 8 * size, tile_body, tuple(jnp.zeros((8, 128), F32) for q in range(25))
+    )
+    for q in range(25):
+        acc[8 * q : 8 * q + 8, :] = sums25[q]
+    for k in range(9):
+        q = 25 + k
+        acc[8 * q : 8 * q + 8, :] = (
+            wall_acc[k, 0] * band_back[k, 0] + wall_acc[k, 1] * band_back[k, 1]
+        )
+    halves = lax.broadcasted_iota(jnp.int32, (128, 128), 0) // 64
+    parity = lax.rem(lax.broadcasted_iota(jnp.int32, (128, 128), 1), 2)
+    lines = dot(acc[...], (halves == parity).astype(F32))
+    total = jnp.zeros((8, 128), F32)
+    for q in range(34):
+        total = jnp.where(lane // 2 == q, lines[8 * q : 8 * q + 8, :], total)
+
+    full_row = lax.broadcasted_iota(jnp.int32, (ROWS, ROWS), 0)
+    full_lane = lax.broadcasted_iota(jnp.int32, (ROWS, ROWS), 1)
+    row_z = lax.rem(full_row, HALF) // 8 * 2 + lax.rem(full_row, 2)
+    matrix = jnp.zeros((ROWS, ROWS), F32)
+    for block in range(BLOCKS):
+        base = 2 + BLOCK * block
+        value = gram[block, 0]
+        for p in range(1, size):
+            value = value + gram[block, p]
+        keep = (row_z == full_lane // 8) & (row_z + base >= 4) & (row_z + base < 4 + OWN)
+        matrix = matrix + jnp.where(keep, value, 0.0)
+    gather = (
+        lax.broadcasted_iota(jnp.int32, (8, ROWS), 0)
+        == lax.rem(lax.broadcasted_iota(jnp.int32, (8, ROWS), 1), 8)
+    ).astype(F32)
+    by_row = dot(gather, matrix, ((1,), (1,)))
+    source_row = lax.broadcasted_iota(jnp.int32, (ROWS, 128), 0)
+    place = 2 * (34 + lax.rem(source_row, 8) // 2) + source_row // HALF
+    place = place == lax.broadcasted_iota(jnp.int32, (ROWS, 128), 1)
+    sums[me] = total + dot(by_row, place.astype(F32))
+
+    def r_copy(step):
+        return remote(sums.at[me], sums.at[me], r_send.at[step], r_recv.at[step], coords(step))
+
+    @pl.loop(1, everyone)
+    def _(step):
+        r_copy(step).start()
+
+    for block in range(BLOCKS):
+        for step in range(1, 2 * size):
+            g_wait(block, step).wait_recv()
+        g_near(block).wait()
+
+    for side in range(2):
+        @pl.loop(0, 64, unroll=8)
+        def _(zp, side=side):
+            at = pl.ds(pl.multiple_of(zp * 16, 16), 16)
+            turn[side, at, :] = ghome[side, zp].astype(F32)
+
+        for cp in range(8):
+            block = turn[side, pl.ds(cp, 128, stride=8), :].T
+            out[pl.ds(side * 16 + 2 * cp, 2)] = block.reshape(2, 64, 128).astype(BF16)
+
+    def r_wait(step):
+        place = lax.rem(me + everyone - step, everyone)
+        return remote(
+            sums.at[place], sums.at[place], r_send.at[step], r_recv.at[step], coords(step)
+        )
+
+    @pl.loop(1, everyone)
+    def _(step):
+        r_wait(step).wait_recv()
+
+    spot = lax.broadcasted_iota(jnp.int32, (128, 128), 0)
+    want = 2 * lax.broadcasted_iota(jnp.int32, (128, 128), 1)
+    red[...] = jnp.zeros((128, 128), F32)
+    for side in range(2):
+        total = sums[side]
+        for member in range(1, size * depth):
+            total = total + sums[2 * member + side]
+        total = total / volume
+        for par in range(2):
+            red[pl.ds(side * 16 + par, 8, stride=2), :] = dot(total, (spot == want + par).astype(F32))
+    turned = red[...].T
+    tile_out[...] = red[0:32, 0:25]
+    wall_out[...] = turned[25:34, 0:32]
+    class_out[...] = turned[34:38, 0:32]
+
+    for piece in range(len(PIECES)):
+        for sx, sc in others:
+            f_far(piece, sx, sc).wait_send()
+    pl.when(gx == 0)(lambda: f_far(0, 0, 0).wait_send())
+    pl.when(gx == size - 1)(lambda: f_far(len(PIECES) - 1, 0, 0).wait_send())
+    for sx in range(size):
+        if sx:
+            l_mid(sx).wait_send()
+            l_edge(sx).wait_send()
+        l_far(sx).wait_send()
+    for block in range(BLOCKS):
+        p_copy(block).wait_send()
+        for step in range(1, 2 * size):
+            g_copy(block, step).wait_send()
+
+    @pl.loop(1, everyone)
+    def _(step):
+        r_copy(step).wait_send()
+
+
+def regional(
+    size, depth, volume,
+    features, labels, grid_index, stretch, tile_filter, wall_filter, class_weight,
+):
+    chans = features.shape[0]
+    levels = stretch.shape[0]
+    everyone = size * depth * 2
+    dma = pltpu.SemaphoreType.DMA
+    vmem = pl.BlockSpec(memory_space=pltpu.VMEM)
+    far = pl.BlockSpec(memory_space=pl.ANY)
+    wide = pltpu.VMEM((2 * size, WIN, 8, 128), F32)
+    block = pltpu.VMEM((BLOCKS, size, ROWS, 256), F32)
+    half = pltpu.VMEM((BLOCKS, size, HALF, 256), F32)
+    grad, tile_grad, wall_grad, class_grad = pl.pallas_call(
+        functools.partial(region_kernel, (size, depth, volume)),
+        out_shape=(
+            jax.ShapeDtypeStruct((chans, 64, 128), BF16),
+            jax.ShapeDtypeStruct((chans, 25), F32),
+            jax.ShapeDtypeStruct((9, chans), F32),
+            jax.ShapeDtypeStruct((4, chans), F32),
+        ),
+        in_specs=[far] * 7,
+        out_specs=(vmem, vmem, vmem, vmem),
+        scratch_shapes=[
+            pltpu.VMEM((chans, 64, 128), BF16),
+            pltpu.VMEM((128, 128), jnp.int32),
+            pltpu.VMEM((1, 64), jnp.int32),
+            pltpu.VMEM((levels, 9), F32),
+            pltpu.VMEM((chans, 25), F32),
+            pltpu.VMEM((9, chans), F32),
+            pltpu.VMEM((4, chans), F32),
+            pltpu.VMEM((3, 1024, 128), F32),
+            pltpu.VMEM((2, 64, 16, 128), BF16),
+            pltpu.VMEM((size, 2, WIN // 2, 16, 128), BF16),
+            pltpu.VMEM((64, 128), F32),
+            pltpu.VMEM((size + 1, 16, 128), BF16),
+            pltpu.VMEM((size, 3, 16, 128), BF16),
+            pltpu.VMEM((size, 3, 16, 128), F32),
+            pltpu.VMEM((size, 24, 128), F32),
+            wide, wide, wide, wide, wide, wide,
+            block, block, half, half,
+            pltpu.VMEM((25, 8, 128), F32),
+            pltpu.VMEM((9, 2, 8, 128), F32),
+            pltpu.VMEM((9, 2, 8, 128), F32),
+            pltpu.VMEM((9, 2, 8, 128), F32),
+            pltpu.VMEM((9, 2, 8, 128), F32),
+            pltpu.VMEM((34 * 8, 128), F32),
+            pltpu.VMEM((BLOCKS, size, ROWS, ROWS), F32),
+            pltpu.VMEM((128, 128), F32),
+            pltpu.VMEM((128, 128), F32),
+            pltpu.VMEM((128, 128), F32),
+            pltpu.VMEM((2 * size, OWN // 2, 16, 128), BF16),
+            pltpu.VMEM((2, 64, 16, 128), BF16),
+            pltpu.VMEM((everyone, 8, 128), F32),
+            pltpu.VMEM((128, 128), F32),
+            dma((7,)),
+            dma((len(PIECES), size, 2)), dma((len(PIECES), size, 2)),
+            dma((3, size)), dma((3, size)),
+            dma((BLOCKS,)), dma((BLOCKS,)),
+            dma((BLOCKS, 2 * size)), dma((BLOCKS, 2 * size)),
+            dma((everyone,)), dma((everyone,)),
+        ],
+        compiler_params=pltpu.CompilerParams(
+            collective_id=0, has_side_effects=True, vmem_limit_bytes=48 * 1024 * 1024
+        ),
+    )(
+        features.reshape(chans, 64, 128), labels.reshape(128, 128), grid_index.reshape(1, 64),
+        stretch, tile_filter, wall_filter.T, class_weight,
+    )
+    return grad.reshape(features.shape), tile_grad, wall_grad.T, class_grad
+
+
 def shards(features, labels, grid_index, stretch, tile_filter, wall_filter, class_weight):
     chans, rows, cells_x, cells_z = features.shape
     size, depth = lax.axis_size("gx"), lax.axis_size("gz")
     volume = labels.shape[0] * cells_x * size * cells_z * depth
     cpg = chans // size
+    if 128 // size == OWN:
+        return regional(
+            size, depth, volume,
+            features, labels, grid_index, stretch, tile_filter, wall_filter, class_weight,
+        )
     chunks = min(4, cpg)
     per_dest = max(cpg // 4, 1) * 8
     xs = 2 * size

time: 68.8 us -> 66.1 us (0.961)
  Pallas kernels: 61.2 us -> 57.8 us
  local copies, waits for them, and re-layouts: 5.72 us -> 7.23 us
  matrix products: 0.87 us -> 0 us
    pallas_call x1, Pallas kernels: 61.2 us -> 57.8 us  [regional(): pl.pallas_call(functools.partial(region_kernel, (size, depth, volume)), o...]
    unnamed x16 -> x18, local copies, waits for them, and re-layouts: 5.72 us -> 7.23 us
    dot_general x1 -> x0, matrix products: 0.87 us -> none  [shards(): bands = jnp.dot(onehot, stretch, precision=lax.Precision.HIGHEST)]
where the time goes in v1:
time: 66.1 us; the launch traced here: 65.7 us
  Pallas kernels  57.8 us (87%)
  local copies, waits for them, and re-layouts  7.23 us (11%)
    pallas_call x1, Pallas kernels, regional(): pl.pallas_call(functools.partial(region_kernel, (size, depth, volume)), o...  57.8 us
    unnamed x18, local copies, waits for them, and re-layouts  7.23 us

profile of v1, /device:TPU:0, one launch (start us, length us, event | category | flops | bytes accessed | tf_op | source)
XLA Modules:
  0.0 65.7 jit_solution(12046117993198766145)
XLA Ops:
  0.6 0.0 copy-start.5
  0.6 0.0 copy-start.6
  0.7 0.7 %copy-done.5 = f32[4,32]{1,0:T(4,128)S(1)} copy-done((f32[4,32]{1,0:T(4,128)S(1)}, f32[4,32]{1,0:T(4,128)}, u32[]{:S(2)}) %copy-start.5) | copy-done | bytes 536
  1.3 0.0 copy-done.6
  1.3 0.0 copy-start
  1.3 1.0 %copy-done = bf16[32,32,2,128]{3,2,1,0:T(2,128)(2,1)S(1)} copy-done((bf16[32,32,2,128]{3,2,1,0:T(2,128)(2,1)S(1)}, bf16[32,32,2,128]{3,2,1,0:T(2,128)(2,1)}, u32[]{:S(2)}) %copy-start) | copy-done | bytes 524312
  2.4 0.0 copy-start.1
  2.4 0.8 %copy-done.1 = s32[64,2,128]{2,1,0:T(2,128)S(1)} copy-done((s32[64,2,128]{2,1,0:T(2,128)S(1)}, s32[64,2,128]{2,1,0:T(2,128)}, u32[]{:S(2)}) %copy-start.1) | copy-done | bytes 65560
  3.2 0.0 copy-start.2
  3.2 0.7 %copy-done.2 = f32[32,25]{1,0:T(8,128)S(1)} copy-done((f32[32,25]{1,0:T(8,128)S(1)}, f32[32,25]{1,0:T(8,128)}, u32[]{:S(2)}) %copy-start.2) | copy-done | bytes 3224
  3.9 0.0 copy-start.3
  3.9 0.7 %copy-done.3 = f32[16,9]{1,0:T(8,128)S(1)} copy-done((f32[16,9]{1,0:T(8,128)S(1)}, f32[16,9]{1,0:T(8,128)}, u32[]{:S(2)}) %copy-start.3) | copy-done | bytes 600
  4.6 0.0 copy-start.4
  4.6 0.7 %copy-done.4 = f32[32,9]{0,1:T(8,128)S(1)} copy-done((f32[32,9]{0,1:T(8,128)S(1)}, f32[32,9]{0,1:T(8,128)}, u32[]{:S(2)}) %copy-start.4) | copy-done | bytes 1176
  5.3 57.8 %shard_map.102 = (bf16[32,64,128]{2,1,0:T(8,128)(2,1)S(1)}, f32[32,25]{1,0:T(8,128)S(1)}, f32[9,32]{1,0:T(8,128)S(1)}, f32[4,32]{1,0:T(4,128)S(1)}) custom-call(bf16[32,64,128]{2,1,0:T(8,128)(2,1)S(1)} %bitcast.6, s32[128,128]{1,0:T(8,128)S(1)} %bitcast.8, s32[1,64]{1,0:T(1,128)S(1)} %bitcast.11, f32[16,9]{1,0:T(8,128)S(1)} %copy-done.3, ...), custom_call_target="tpu_custom_call" | custom-call | tf_op jit(solution)/shard_map/pallas_call | solution.py:1058
  63.1 0.8 %copy.15 = bf16[32,32,2,128]{3,2,1,0:T(2,128)(2,1)} copy(bf16[32,32,2,128]{3,2,1,0:T(2,128)(2,1)S(1)} %bitcast.7) | data formatting | bytes 1048576
  63.9 0.6 copy.16
  64.5 0.6 copy.17
  65.1 0.6 copy.18
Async XLA Ops:
  0.6 0.7 %copy-start.5 = (f32[4,32]{1,0:T(4,128)S(1)}, f32[4,32]{1,0:T(4,128)}, u32[]{:S(2)}) copy-start(f32[4,32]{1,0:T(4,128)} %class_h.1) | copy-start | bytes 1540
  0.6 0.7 %copy-start.6 = (s32[64]{0:T(128)S(1)}, s32[64]{0:T(128)}, u32[]{:S(2)}) copy-start(s32[64]{0:T(128)} %param.9) | copy-start | bytes 772
  1.3 1.0 %copy-start = (bf16[32,32,2,128]{3,2,1,0:T(2,128)(2,1)S(1)}, bf16[32,32,2,128]{3,2,1,0:T(2,128)(2,1)}, u32[]{:S(2)}) copy-start(bf16[32,32,2,128]{3,2,1,0:T(2,128)(2,1)} %param.7) | copy-start | bytes 1572868
  2.4 0.8 %copy-start.1 = (s32[64,2,128]{2,1,0:T(2,128)S(1)}, s32[64,2,128]{2,1,0:T(2,128)}, u32[]{:S(2)}) copy-start(s32[64,2,128]{2,1,0:T(2,128)} %param.8) | copy-start | bytes 196612
  3.2 0.7 %copy-start.2 = (f32[32,25]{1,0:T(8,128)S(1)}, f32[32,25]{1,0:T(8,128)}, u32[]{:S(2)}) copy-start(f32[32,25]{1,0:T(8,128)} %tile_h.1) | copy-start | bytes 9604
  3.9 0.7 %copy-start.3 = (f32[16,9]{1,0:T(8,128)S(1)}, f32[16,9]{1,0:T(8,128)}, u32[]{:S(2)}) copy-start(f32[16,9]{1,0:T(8,128)} %stretch_h.1) | copy-start | bytes 1732
  4.6 0.7 %copy-start.4 = (f32[32,9]{0,1:T(8,128)S(1)}, f32[32,9]{0,1:T(8,128)}, u32[]{:S(2)}) copy-start(f32[32,9]{0,1:T(8,128)} %param.12) | copy-start | bytes 3460

commit v2 on v1

--- a/solution.py
+++ b/solution.py
@@ -443,6 +443,18 @@
 HIGH = lax.Precision.HIGHEST
 
 
+def cast_dot(a, b, dims=((1,), (0,))):
+    return lax.dot_general(
+        a.astype(BF16), b.astype(BF16), (dims, ((), ())), preferred_element_type=F32
+    )
+
+
+def split_dot(a, b):
+    a_high, b_high = a.astype(BF16), b.astype(BF16)
+    a_low, b_low = (a - a_high.astype(F32)).astype(BF16), (b - b_high.astype(F32)).astype(BF16)
+    return cast_dot(a_high, b_high) + (cast_dot(a_high, b_low) + cast_dot(a_low, b_high))
+
+
 def dot(a, b, dims=((1,), (0,))):
     return lax.dot_general(a, b, (dims, ((), ())), precision=HIGH, preferred_element_type=F32)
 
@@ -454,7 +466,7 @@
     feat, lab, index, stretch, tile_w, wall_w, class_w,
     turn, send, recv, lab_rows, lab_send, lab_recv, lab_wide, lab_win,
     field, odd, smooth, gwall, gsm, godd, hid, slope, part_out, part_in,
-    taps, fore, back, band_back, wall_acc, acc, gram, params, classes, classes_t,
+    taps, fore, wide, wide_t, band_tile, wall, wall_acc, acc, gram, params, classes, classes_t,
     gout, ghome, sums, red,
     in_sem, f_send, f_recv, l_send, l_recv, p_send, p_recv, g_send, g_recv, r_send, r_recv,
 ):
@@ -646,17 +658,48 @@
     band_t = params[32:48, 0:64]
     y_row = lax.broadcasted_iota(jnp.int32, (64, 128), 0)
     y_col = lax.rem(lax.broadcasted_iota(jnp.int32, (64, 128), 1), 64) // 2
+    square_row = lax.broadcasted_iota(jnp.int32, (128, 128), 0)
+    square_lane = lax.broadcasted_iota(jnp.int32, (128, 128), 1)
+    k_of_lane = lax.rem(lax.broadcasted_iota(jnp.int32, (16, 128), 1) // 2 + 4, 64)
+    k_of_lane = (k_of_lane == lax.broadcasted_iota(jnp.int32, (16, 128), 0)) & (
+        lax.rem(lax.broadcasted_iota(jnp.int32, (16, 128), 1), 2) == 0
+    )
+    placed = dot(band_t, k_of_lane.astype(F32), ((0,), (0,)))
     for yh in range(2):
         ahead = dot(band_t, (y_row == y_col + 32 * yh).astype(F32))
         for k in range(9):
             m = k - 4
-            weight = spread(wall_pairs, k)
-            inside = (y_lane + (32 * yh + m) >= 0) & (y_lane + (32 * yh + m) < 64)
-            fore[k, yh] = jnp.where(inside, weight * ahead[k : k + 1, :], 0.0)
-            behind = dot(band_t, (y_row == y_col + (32 * yh - m)).astype(F32))
-            band_back[k, yh] = jnp.broadcast_to(behind[k : k + 1, :], (8, 128))
-            back[k, yh] = weight * band_back[k, yh]
-            wall_acc[k, yh] = jnp.zeros((8, 128), F32)
+            value = spread(wall_pairs, k) * ahead[k : k + 1, :]
+            inside = (y_lane + m >= 0) & (y_lane + m < 32)
+            fore[k, yh] = jnp.where(inside, value, 0.0)
+            across = (y_lane + m >= 32) if yh == 0 else (y_lane + m < 0)
+            fore[k, 2 + yh] = jnp.where(across, value, 0.0)
+        rows_y = lax.broadcasted_iota(jnp.int32, (128, 64), 0) % 64 // 2 + 32 * yh
+        at_y = rows_y == lax.broadcasted_iota(jnp.int32, (128, 64), 1)
+        value = dot(at_y.astype(F32), placed)
+        shift = lax.rem(square_lane // 2 + 4, 64) - 4 + square_row % 64 // 2
+        inner = jnp.where((shift >= 0) & (shift < 32), value, 0.0)
+        outer = jnp.where((shift >= 0) & (shift < 32), 0.0, value)
+        band_tile[yh] = pltpu.roll(inner, 0, 1, stride=1, stride_axis=0)
+        band_tile[2 + yh] = pltpu.roll(outer, 64, 1, stride=1, stride_axis=0)
+
+    @pl.loop(0, 8, unroll=2)
+    def _(cp):
+        for yh in range(2):
+            tile = jnp.zeros((128, 128), F32)
+            for k in range(9):
+                line = fore[k, yh, pl.ds(cp, 1), :]
+                tile = jnp.where(square_row == square_lane + 2 * (k - 4), line, tile)
+            wide[cp, 128 * yh : 128 * yh + 128, 128 * yh : 128 * yh + 128] = tile.astype(BF16)
+            wide_t[cp, 128 * yh : 128 * yh + 128, 128 * yh : 128 * yh + 128] = tile.T.astype(BF16)
+            tile = jnp.zeros((128, 128), F32)
+            for k in range(5, 9) if yh == 0 else range(4):
+                line = fore[k, 2 + yh, pl.ds(cp, 1), :]
+                far = 2 * (k - 4) - 64 if yh == 0 else 2 * (k - 4) + 64
+                tile = jnp.where(square_row == square_lane + far, line, tile)
+            low, high = 128 - 128 * yh, 128 * yh
+            wide[cp, low : low + 128, high : high + 128] = tile.astype(BF16)
+            wide_t[cp, high : high + 128, low : low + 128] = tile.T.astype(BF16)
 
     chan = lax.broadcasted_iota(jnp.int32, (128, 128), 0)
     unit = lax.rem(lax.broadcasted_iota(jnp.int32, (128, 128), 1), 8)
@@ -691,7 +734,13 @@
                 field[t, 2 * zp] = pair[0:8]
                 field[t, 2 * zp + 1] = pair[8:16]
 
-        between(field, odd, 2 * low, 2 * high)
+        between(seen(field), odd, 2 * low, 2 * high)
+
+    def seen(ref):
+        return lambda t, z: ref[t, z]
+
+    def seen_rows(ref):
+        return lambda t, z: ref[lax.rem(t, 2), spot(z, t // 2), :]
 
     def between(src, dst, low, high):
         @pl.loop(0, 2 * size)
@@ -699,7 +748,7 @@
             after = lax.rem(t + 2, 2 * size)
             for z in range(low, high):
                 dst[t, z] = jnp.where(
-                    x_even, pltpu.roll(src[t, z], 127, 1), pltpu.roll(src[after, z], 1, 1)
+                    x_even, pltpu.roll(src(t, z), 127, 1), pltpu.roll(src(after, z), 1, 1)
                 )
 
     def filtered(src, mid, t, low, count, flip, put):
@@ -707,7 +756,7 @@
         totals = [None] * count
         for z in range(count + 4):
             at = low + z - 2
-            views = (src[before, at], mid[before, at], src[t, at], mid[t, at], src[after, at])
+            views = (src(before, at), mid[before, at], src(t, at), mid[t, at], src(after, at))
             for j in range(5):
                 if 0 <= z - j < count:
                     for i in range(5):
@@ -718,14 +767,15 @@
             if z >= 4:
                 put(z - 4, totals)
 
-    def moved(low, high, low_turned, high_turned, m):
-        if m == 0:
-            return low, high
-        if m > 0:
-            mixed = jnp.where(y_lane < m, high_turned, low)
-            return pltpu.roll(mixed, 128 - 2 * m, 1), pltpu.roll(high, 128 - 2 * m, 1)
-        mixed = jnp.where(y_lane >= 32 + m, low_turned, high)
-        return pltpu.roll(low, -2 * m, 1), pltpu.roll(mixed, -2 * m, 1)
+    def spot(z, p):
+        return pl.ds(pl.multiple_of((z * size + p) * 8, 8), 8)
+
+    def unit_rows(z, count, cp):
+        return pl.ds(z * size * 8 + cp, count * size, stride=8)
+
+    def unit_of(ref, z, count, cp):
+        at = unit_rows(z, count, cp)
+        return jnp.concatenate([ref[0, at, :], ref[1, at, :]], axis=1).astype(BF16)
 
     def p_copy(block):
         return remote(
@@ -739,33 +789,34 @@
         @pl.loop(0, 2 * size)
         def _(t):
             def put(z, totals):
-                smooth[t, base + z] = rounded(totals[z])
-
-            filtered(field, odd, t, base, BLOCK, False, put)
+                smooth[lax.rem(t, 2), spot(base + z, t // 2), :] = rounded(totals[z])
+
+            filtered(seen(field), odd, t, base, BLOCK, False, put)
+
+        @pl.loop(0, 8, unroll=8)
+        def _(cp):
+            both = jnp.dot(
+                unit_of(smooth, base, BLOCK, cp), wide[cp], preferred_element_type=F32
+            )
+            for yh in range(2):
+                wall[yh, unit_rows(0, BLOCK, cp), :] = both[:, 128 * yh : 128 * yh + 128]
 
         @pl.loop(0, BLOCK)
         def _(z):
             at = pl.ds(pl.multiple_of(8 * z, 8), 8)
             for p in range(size):
-                low, high = smooth[2 * p, base + z], smooth[2 * p + 1, base + z]
-                turned = pltpu.roll(low, 64, 1), pltpu.roll(high, 64, 1)
-                walls = [None, None]
-                for k in range(9):
-                    pair = moved(low, high, *turned, k - 4)
-                    for yh in range(2):
-                        term = fore[k, yh] * pair[yh]
-                        walls[yh] = term if walls[yh] is None else walls[yh] + term
-                for yh, wall in enumerate(walls):
-                    sig = jax.nn.sigmoid(wall)
+                for yh in range(2):
+                    value = wall[yh, spot(z, p), :]
+                    sig = jax.nn.sigmoid(value)
                     lanes = slice(128 * yh, 128 * yh + 128)
-                    hid[block, p, at, lanes] = wall * sig
-                    slope[block, p, at, lanes] = sig * (1.0 + wall * (1.0 - sig))
+                    hid[block, p, at, lanes] = value * sig
+                    slope[block, p, at, lanes] = sig * (1.0 + value * (1.0 - sig))
 
         left_half = lax.rem(lax.broadcasted_iota(jnp.int32, (HALF, 256), 1), 128) < 64
 
-        @pl.loop(0, size)
+        @pl.loop(0, size, unroll=size)
         def _(p):
-            part = dot(classes[0:ROWS, 0:ROWS], hid[block, p])
+            part = split_dot(classes[0:ROWS, 0:ROWS], hid[block, p])
             part_out[block, p] = jnp.where(left_half, part[0:HALF], part[HALF:ROWS])
             lanes = pl.ds(pl.multiple_of(128 * col, 128), 128)
             for zp in range(BLOCK // 2):
@@ -783,7 +834,7 @@
         p_copy(block).wait_recv()
         left_half = lax.rem(lax.broadcasted_iota(jnp.int32, (HALF, 256), 1), 128) < 64
 
-        @pl.loop(0, size)
+        @pl.loop(0, size, unroll=size)
         def _(p):
             err = part_out[block, p] + part_in[block, p]
             swapped = jnp.concatenate(
@@ -793,41 +844,25 @@
             both = jnp.concatenate(
                 [jnp.where(left_half, err, 0.0), jnp.where(left_half, 0.0, err)], axis=0
             )
-            grad = dot(classes_t[0:ROWS, 0:ROWS], both) * slope[block, p]
+            grad = split_dot(classes_t[0:ROWS, 0:ROWS], both) * slope[block, p]
             for z in range(BLOCK):
                 for yh in range(2):
-                    gwall[2 * p + yh, base + z] = rounded(
+                    gwall[yh, spot(base + z, p), :] = rounded(
                         grad[8 * z : 8 * z + 8, 128 * yh : 128 * yh + 128]
                     )
-            new = dot(both, hid[block, p], ((1,), (1,)))
+            new = cast_dot(both, hid[block, p], ((1,), (1,)))
             gram[block, p] = new
 
-        @pl.loop(0, BLOCK)
-        def _(z):
-            own = (base + z >= 4) & (base + z < 4 + OWN)
-            sums9 = [[None, None] for k in range(9)]
-            for p in range(size):
-                low, high = gwall[2 * p, base + z], gwall[2 * p + 1, base + z]
-                turned = pltpu.roll(low, 64, 1), pltpu.roll(high, 64, 1)
-                fields = [
-                    jnp.where(own, smooth[2 * p + yh, base + z], 0.0) for yh in range(2)
-                ]
-                totals = [None, None]
-                for k in range(9):
-                    pair = moved(low, high, *turned, 4 - k)
-                    for yh in range(2):
-                        term = back[k, yh] * pair[yh]
-                        totals[yh] = term if totals[yh] is None else totals[yh] + term
-                        term = pair[yh] * fields[yh]
-                        old = sums9[k][yh]
-                        sums9[k][yh] = term if old is None else old + term
-                for yh in range(2):
-                    gsm[2 * p + yh, base + z] = rounded(totals[yh])
-            for k in range(9):
-                for yh in range(2):
-                    wall_acc[k, yh] = wall_acc[k, yh] + sums9[k][yh]
-
-        between(gsm, godd, base, base + BLOCK)
+        @pl.loop(0, 8, unroll=8)
+        def _(cp):
+            both = jnp.dot(
+                unit_of(gwall, base, BLOCK, cp), wide_t[cp], preferred_element_type=F32
+            )
+            for yh in range(2):
+                at = unit_rows(base, BLOCK, cp)
+                gsm[yh, at, :] = rounded(both[:, 128 * yh : 128 * yh + 128])
+
+        between(seen_rows(gsm), godd, base, base + BLOCK)
 
     def g_spot(block):
         low = 4 if block == 0 else BLOCK * block
@@ -874,7 +909,7 @@
                     pair = jnp.concatenate([totals[z - 1], totals[z]], axis=0)
                     gout[t, (low - 4 + z) // 2] = pair.astype(BF16)
 
-            filtered(gsm, godd, t, low, count, True, put)
+            filtered(seen_rows(gsm), godd, t, low, count, True, put)
 
             @pl.when(step > 0)
             def _():
@@ -924,7 +959,7 @@
     def tile_body(it, sums25):
         t, base = it // 4, 4 + 8 * lax.rem(it, 4)
         before, after = lax.rem(t + 2 * size - 2, 2 * size), lax.rem(t + 2, 2 * size)
-        grads = [gsm[t, base + z] for z in range(8)]
+        grads = [seen_rows(gsm)(t, base + z) for z in range(8)]
         news = list(sums25)
         for z in range(12):
             at = base + z - 2
@@ -942,16 +977,29 @@
     )
     for q in range(25):
         acc[8 * q : 8 * q + 8, :] = sums25[q]
-    for k in range(9):
-        q = 25 + k
-        acc[8 * q : 8 * q + 8, :] = (
-            wall_acc[k, 0] * band_back[k, 0] + wall_acc[k, 1] * band_back[k, 1]
-        )
+
+    @pl.loop(0, 8, unroll=8)
+    def _(cp):
+        grads, fields = unit_of(gwall, 4, OWN, cp), unit_of(smooth, 4, OWN, cp)
+        both = cast_dot(grads, fields, ((0,), (0,)))
+        for par in range(2):
+            wall_acc[par, cp] = jnp.zeros((8, 128), F32)
+        for yh in range(2):
+            here, far = slice(128 * yh, 128 * yh + 128), slice(128 - 128 * yh, 256 - 128 * yh)
+            for g in range(16):
+                at = slice(128 * yh + 8 * g, 128 * yh + 8 * g + 8)
+                tile = both[at, here] * band_tile[yh, 8 * g : 8 * g + 8, :]
+                if g % 8 == (0 if yh else 7):
+                    edge = both[at, far] * band_tile[2 + yh, 8 * g : 8 * g + 8, :]
+                    tile = tile + pltpu.roll(edge, 64, 1)
+                wall_acc[g // 8, cp] = wall_acc[g // 8, cp] + pltpu.roll(tile, (128 - 8 * g) % 128, 1)
+
+    inner_row = lax.rem(lax.broadcasted_iota(jnp.int32, (64, 128), 0), 8)
     halves = lax.broadcasted_iota(jnp.int32, (128, 128), 0) // 64
     parity = lax.rem(lax.broadcasted_iota(jnp.int32, (128, 128), 1), 2)
     lines = dot(acc[...], (halves == parity).astype(F32))
     total = jnp.zeros((8, 128), F32)
-    for q in range(34):
+    for q in range(25):
         total = jnp.where(lane // 2 == q, lines[8 * q : 8 * q + 8, :], total)
 
     full_row = lax.broadcasted_iota(jnp.int32, (ROWS, ROWS), 0)
@@ -973,7 +1021,22 @@
     source_row = lax.broadcasted_iota(jnp.int32, (ROWS, 128), 0)
     place = 2 * (34 + lax.rem(source_row, 8) // 2) + source_row // HALF
     place = place == lax.broadcasted_iota(jnp.int32, (ROWS, 128), 1)
-    sums[me] = total + dot(by_row, place.astype(F32))
+    total = total + dot(by_row, place.astype(F32))
+    stack = (
+        lax.broadcasted_iota(jnp.int32, (8, 64), 0)
+        == lax.broadcasted_iota(jnp.int32, (8, 64), 1) // 8
+    ).astype(F32)
+    for par in range(2):
+        value = wall_acc[par].reshape(64, 128)
+        for r in range(1, 8):
+            value = jnp.where(inner_row == r, pltpu.roll(value, 128 - r, 1), value)
+        by_lane = dot(stack, value)
+        source = lax.rem(square_row // 2 + 4, 64)
+        place = (lax.rem(square_row, 2) == 0) & (source < 9) & (
+            square_lane == 2 * (25 + source) + par
+        )
+        total = total + dot(by_lane, place.astype(F32))
+    sums[me] = total
 
     def r_copy(step):
         return remote(sums.at[me], sums.at[me], r_send.at[step], r_recv.at[step], coords(step))
@@ -1053,6 +1116,7 @@
     vmem = pl.BlockSpec(memory_space=pltpu.VMEM)
     far = pl.BlockSpec(memory_space=pl.ANY)
     wide = pltpu.VMEM((2 * size, WIN, 8, 128), F32)
+    rows = pltpu.VMEM((2, WIN * size * 8, 128), F32)
     block = pltpu.VMEM((BLOCKS, size, ROWS, 256), F32)
     half = pltpu.VMEM((BLOCKS, size, HALF, 256), F32)
     grad, tile_grad, wall_grad, class_grad = pl.pallas_call(
@@ -1081,14 +1145,16 @@
             pltpu.VMEM((size, 3, 16, 128), BF16),
             pltpu.VMEM((size, 3, 16, 128), F32),
             pltpu.VMEM((size, 24, 128), F32),
-            wide, wide, wide, wide, wide, wide,
+            wide, wide, rows, rows, rows, wide,
             block, block, half, half,
             pltpu.VMEM((25, 8, 128), F32),
-            pltpu.VMEM((9, 2, 8, 128), F32),
-            pltpu.VMEM((9, 2, 8, 128), F32),
-            pltpu.VMEM((9, 2, 8, 128), F32),
-            pltpu.VMEM((9, 2, 8, 128), F32),
-            pltpu.VMEM((34 * 8, 128), F32),
+            pltpu.VMEM((9, 4, 8, 128), F32),
+            pltpu.VMEM((8, 256, 256), BF16),
+            pltpu.VMEM((8, 256, 256), BF16),
+            pltpu.VMEM((4, 128, 128), F32),
+            pltpu.VMEM((2, ROWS * size, 128), F32),
+            pltpu.VMEM((2, 8, 8, 128), F32),
+            pltpu.VMEM((25 * 8, 128), F32),
             pltpu.VMEM((BLOCKS, size, ROWS, ROWS), F32),
             pltpu.VMEM((128, 128), F32),
             pltpu.VMEM((128, 128), F32),
@@ -1105,7 +1171,7 @@
             dma((everyone,)), dma((everyone,)),
         ],
         compiler_params=pltpu.CompilerParams(
-            collective_id=0, has_side_effects=True, vmem_limit_bytes=48 * 1024 * 1024
+            collective_id=0, has_side_effects=True, vmem_limit_bytes=63 * 1024 * 1024
         ),
     )(
         features.reshape(chans, 64, 128), labels.reshape(128, 128), grid_index.reshape(1, 64),

time: 66.1 us -> 50.1 us (0.76)
  Pallas kernels: 57.8 us -> 45 us
  local copies, waits for them, and re-layouts: 7.23 us -> 4.23 us
    pallas_call x1, Pallas kernels: 57.8 us -> 45 us  [regional(): pl.pallas_call(functools.partial(region_kernel, (size, depth, volume)), o...]
    unnamed x18 -> x10, local copies, waits for them, and re-layouts: 7.23 us -> 4.23 us
where the time goes in v2:
time: 50.1 us; the launch traced here: 49.9 us
  Pallas kernels  45 us (90%)
  local copies, waits for them, and re-layouts  4.23 us (8%)
  between operations  0.65 us (1%)
    pallas_call x1, Pallas kernels, regional(): pl.pallas_call(functools.partial(region_kernel, (size, depth, volume)), o...  45 us
    unnamed x10, local copies, waits for them, and re-layouts  4.23 us

profile of v2, /device:TPU:0, one launch (start us, length us, event | category | flops | bytes accessed | tf_op | source)
XLA Modules:
  0.0 49.9 jit_solution(14047003557908102997)
XLA Ops:
  0.6 45.0 %shard_map.102 = (bf16[32,64,128]{2,1,0:T(8,128)(2,1)}, f32[32,25]{1,0:T(8,128)}, f32[9,32]{1,0:T(8,128)}, f32[4,32]{1,0:T(4,128)}) custom-call(bf16[32,64,128]{2,1,0:T(8,128)(2,1)} %bitcast.6, s32[128,128]{1,0:T(8,128)} %bitcast.8, s32[1,64]{1,0:T(1,128)} %bitcast.11, f32[16,9]{1,0:T(8,128)} %stretch_h.1, f32[32,25]{1,0:T(8,128)} %tile_h.1, ...), custom_call_target="tpu_custom_call" | custom-call | tf_op jit(solution)/shard_map/pallas_call | solution.py:1122
  45.6 0.0 copy-start
  45.6 2.3 %copy.15 = bf16[32,32,2,128]{3,2,1,0:T(2,128)(2,1)} copy(bf16[32,32,2,128]{3,2,1,0:T(2,128)(2,1)} %bitcast.7) | data formatting | bytes 1048576
  47.9 0.0 copy-done
  47.9 0.0 copy-start.1
  47.9 0.6 %copy.16 = f32[32,25]{1,0:T(8,128)} copy(f32[32,25]{1,0:T(8,128)S(1)} %copy-done) | data formatting | bytes 6400
  48.5 0.1 copy-done.1
  48.6 0.0 copy-start.2
  48.6 0.6 %copy.17 = f32[32,9]{0,1:T(8,128)} copy(f32[32,9]{0,1:T(8,128)S(1)} %bitcast.10) | data formatting | bytes 2304
  49.2 0.1 copy-done.2
  49.3 0.6 %copy.18 = f32[4,32]{1,0:T(4,128)} copy(f32[4,32]{1,0:T(4,128)S(1)} %copy-done.2) | data formatting | bytes 1024
Async XLA Ops:
  45.6 2.3 %copy-start = (f32[32,25]{1,0:T(8,128)S(1)}, f32[32,25]{1,0:T(8,128)}, u32[]{:S(2)}) copy-start(f32[32,25]{1,0:T(8,128)} %get-tuple-element.17) | copy-start | bytes 9604
  47.9 0.7 %copy-start.1 = (f32[9,32]{1,0:T(8,128)S(1)}, f32[9,32]{1,0:T(8,128)}, u32[]{:S(2)}) copy-start(f32[9,32]{1,0:T(8,128)} %get-tuple-element.10) | copy-start | bytes 3460
  48.6 0.7 %copy-start.2 = (f32[4,32]{1,0:T(4,128)S(1)}, f32[4,32]{1,0:T(4,128)}, u32[]{:S(2)}) copy-start(f32[4,32]{1,0:T(4,128)} %get-tuple-element.19) | copy-start | bytes 1540

commit v3 on v2

--- a/solution.py
+++ b/solution.py
@@ -462,12 +462,12 @@
 def region_kernel(
     dims,
     feat_h, lab_h, index_h, stretch_h, tile_h, wall_h, class_h,
-    out, tile_out, wall_out, class_out,
+    ghome, sums,
     feat, lab, index, stretch, tile_w, wall_w, class_w,
     turn, send, recv, lab_rows, lab_send, lab_recv, lab_wide, lab_win,
     field, odd, smooth, gwall, gsm, godd, hid, slope, part_out, part_in,
     taps, fore, wide, wide_t, band_tile, wall, wall_acc, acc, gram, params, classes, classes_t,
-    gout, ghome, sums, red,
+    gout, mine, red,
     in_sem, f_send, f_recv, l_send, l_recv, p_send, p_recv, g_send, g_recv, r_send, r_recv,
 ):
     size, depth, volume = dims
@@ -1036,10 +1036,13 @@
             square_lane == 2 * (25 + source) + par
         )
         total = total + dot(by_lane, place.astype(F32))
-    sums[me] = total
+    mine[...] = total
 
     def r_copy(step):
-        return remote(sums.at[me], sums.at[me], r_send.at[step], r_recv.at[step], coords(step))
+        return remote(mine, sums.at[me], r_send.at[step], r_recv.at[step], coords(step))
+
+    r_own = pltpu.make_async_copy(mine, sums.at[me], r_recv.at[0])
+    r_own.start()
 
     @pl.loop(1, everyone)
     def _(step):
@@ -1050,16 +1053,6 @@
             g_wait(block, step).wait_recv()
         g_near(block).wait()
 
-    for side in range(2):
-        @pl.loop(0, 64, unroll=8)
-        def _(zp, side=side):
-            at = pl.ds(pl.multiple_of(zp * 16, 16), 16)
-            turn[side, at, :] = ghome[side, zp].astype(F32)
-
-        for cp in range(8):
-            block = turn[side, pl.ds(cp, 128, stride=8), :].T
-            out[pl.ds(side * 16 + 2 * cp, 2)] = block.reshape(2, 64, 128).astype(BF16)
-
     def r_wait(step):
         place = lax.rem(me + everyone - step, everyone)
         return remote(
@@ -1070,21 +1063,7 @@
     def _(step):
         r_wait(step).wait_recv()
 
-    spot = lax.broadcasted_iota(jnp.int32, (128, 128), 0)
-    want = 2 * lax.broadcasted_iota(jnp.int32, (128, 128), 1)
-    red[...] = jnp.zeros((128, 128), F32)
-    for side in range(2):
-        total = sums[side]
-        for member in range(1, size * depth):
-            total = total + sums[2 * member + side]
-        total = total / volume
-        for par in range(2):
-            red[pl.ds(side * 16 + par, 8, stride=2), :] = dot(total, (spot == want + par).astype(F32))
-    turned = red[...].T
-    tile_out[...] = red[0:32, 0:25]
-    wall_out[...] = turned[25:34, 0:32]
-    class_out[...] = turned[34:38, 0:32]
-
+    r_own.wait()
     for piece in range(len(PIECES)):
         for sx, sc in others:
             f_far(piece, sx, sc).wait_send()
@@ -1105,6 +1084,39 @@
         r_copy(step).wait_send()
 
 
+def last_kernel(volume, home, sums, out, tile_out, wall_out, class_out, turn, red):
+    side = pl.program_id(0)
+    members = sums.shape[0] // 2
+
+    @pl.loop(0, 64, unroll=8)
+    def _(zp):
+        at = pl.ds(pl.multiple_of(zp * 16, 16), 16)
+        turn[at, :] = home[0, zp].astype(F32)
+
+    for cp in range(8):
+        block = turn[pl.ds(cp, 128, stride=8), :].T
+        out[pl.ds(2 * cp, 2)] = block.reshape(2, 64, 128).astype(BF16)
+
+    @pl.when(side == 0)
+    def _():
+        spot = lax.broadcasted_iota(jnp.int32, (128, 128), 0)
+        want = 2 * lax.broadcasted_iota(jnp.int32, (128, 128), 1)
+        red[...] = jnp.zeros((128, 128), F32)
+        for half in range(2):
+            total = sums[half]
+            for member in range(1, members):
+                total = total + sums[2 * member + half]
+            total = total / volume
+            for par in range(2):
+                red[pl.ds(half * 16 + par, 8, stride=2), :] = dot(
+                    total, (spot == want + par).astype(F32)
+                )
+        turned = red[...].T
+        tile_out[...] = red[0:32, 0:25]
+        wall_out[...] = turned[25:34, 0:32]
+        class_out[...] = turned[34:38, 0:32]
+
+
 def regional(
     size, depth, volume,
     features, labels, grid_index, stretch, tile_filter, wall_filter, class_weight,
@@ -1113,22 +1125,19 @@
     levels = stretch.shape[0]
     everyone = size * depth * 2
     dma = pltpu.SemaphoreType.DMA
-    vmem = pl.BlockSpec(memory_space=pltpu.VMEM)
     far = pl.BlockSpec(memory_space=pl.ANY)
     wide = pltpu.VMEM((2 * size, WIN, 8, 128), F32)
     rows = pltpu.VMEM((2, WIN * size * 8, 128), F32)
     block = pltpu.VMEM((BLOCKS, size, ROWS, 256), F32)
     half = pltpu.VMEM((BLOCKS, size, HALF, 256), F32)
-    grad, tile_grad, wall_grad, class_grad = pl.pallas_call(
+    home, sums = pl.pallas_call(
         functools.partial(region_kernel, (size, depth, volume)),
         out_shape=(
-            jax.ShapeDtypeStruct((chans, 64, 128), BF16),
-            jax.ShapeDtypeStruct((chans, 25), F32),
-            jax.ShapeDtypeStruct((9, chans), F32),
-            jax.ShapeDtypeStruct((4, chans), F32),
+            jax.ShapeDtypeStruct((2, 64, 16, 128), BF16),
+            jax.ShapeDtypeStruct((everyone, 8, 128), F32),
         ),
         in_specs=[far] * 7,
-        out_specs=(vmem, vmem, vmem, vmem),
+        out_specs=(far, far),
         scratch_shapes=[
             pltpu.VMEM((chans, 64, 128), BF16),
             pltpu.VMEM((128, 128), jnp.int32),
@@ -1160,8 +1169,7 @@
             pltpu.VMEM((128, 128), F32),
             pltpu.VMEM((128, 128), F32),
             pltpu.VMEM((2 * size, OWN // 2, 16, 128), BF16),
-            pltpu.VMEM((2, 64, 16, 128), BF16),
-            pltpu.VMEM((everyone, 8, 128), F32),
+            pltpu.VMEM((8, 128), F32),
             pltpu.VMEM((128, 128), F32),
             dma((7,)),
             dma((len(PIECES), size, 2)), dma((len(PIECES), size, 2)),
@@ -1177,6 +1185,28 @@
         features.reshape(chans, 64, 128), labels.reshape(128, 128), grid_index.reshape(1, 64),
         stretch, tile_filter, wall_filter.T, class_weight,
     )
+    def whole(*shape):
+        return pl.BlockSpec(shape, lambda side: (0,) * len(shape))
+
+    grad, tile_grad, wall_grad, class_grad = pl.pallas_call(
+        functools.partial(last_kernel, volume),
+        grid=(2,),
+        out_shape=(
+            jax.ShapeDtypeStruct((chans, 64, 128), BF16),
+            jax.ShapeDtypeStruct((chans, 25), F32),
+            jax.ShapeDtypeStruct((9, chans), F32),
+            jax.ShapeDtypeStruct((4, chans), F32),
+        ),
+        in_specs=[
+            pl.BlockSpec((1, 64, 16, 128), lambda side: (side, 0, 0, 0)),
+            whole(everyone, 8, 128),
+        ],
+        out_specs=(
+            pl.BlockSpec((chans // 2, 64, 128), lambda side: (side, 0, 0)),
+            whole(chans, 25), whole(9, chans), whole(4, chans),
+        ),
+        scratch_shapes=[pltpu.VMEM((1024, 128), F32), pltpu.VMEM((128, 128), F32)],
+    )(home, sums)
     return grad.reshape(features.shape), tile_grad, wall_grad.T, class_grad
 
 

time: 50.1 us -> 47 us (0.938)
  local copies, waits for them, and re-layouts: 4.23 us -> 0 us
  Pallas kernels: 45 us -> 46.2 us
    unnamed x10 -> x0, local copies, waits for them, and re-layouts: 4.23 us -> none
    pallas_call x0 -> x1, Pallas kernels: none -> 2.46 us  [regional(): pl.pallas_call(functools.partial(last_kernel, volume), grid=(2,), out_sha...]
    pallas_call x1, Pallas kernels: 45 us -> 43.7 us  [regional(): pl.pallas_call(functools.partial(region_kernel, (size, depth, volume)), o...]
where the time goes in v3:
time: 47 us; the launch traced here: 46.8 us
  Pallas kernels  46.2 us (98%)
  between operations  0.64 us (1%)
    pallas_call x1, Pallas kernels, regional(): pl.pallas_call(functools.partial(region_kernel, (size, depth, volume)), o...  43.7 us
    pallas_call x1, Pallas kernels, regional(): pl.pallas_call(functools.partial(last_kernel, volume), grid=(2,), out_sha...  2.46 us

profile of v3, /device:TPU:0, one launch (start us, length us, event | category | flops | bytes accessed | tf_op | source)
XLA Modules:
  0.0 46.8 jit_solution(14039762391598490176)
XLA Ops:
  0.6 43.7 %shard_map.102 = (bf16[2,64,16,128]{3,2,1,0:T(8,128)(2,1)}, f32[16,8,128]{2,1,0:T(8,128)}) custom-call(bf16[32,64,128]{2,1,0:T(8,128)(2,1)} %bitcast.6, s32[128,128]{1,0:T(8,128)} %bitcast.7, s32[1,64]{1,0:T(1,128)} %bitcast.9, f32[16,9]{1,0:T(8,128)} %stretch_h.1, f32[32,25]{1,0:T(8,128)} %tile_h.1, f32[9,32]{1,0:T(8,128)} %bitcast.8, f32[4,32]{1,0:T(4,128)} %class_h.1), custom_call_target="tpu_custom_call" | custom-call | tf_op jit(solution)/shard_map/pallas_call | solution.py:1133
  44.4 2.5 %shard_map.103 = (bf16[32,64,128]{2,1,0:T(8,128)(2,1)}, f32[32,25]{1,0:T(8,128)}, f32[9,32]{1,0:T(8,128)}, f32[4,32]{1,0:T(4,128)}) custom-call(bf16[2,64,16,128]{3,2,1,0:T(8,128)(2,1)} %get-tuple-element.10.home, f32[16,8,128]{2,1,0:T(8,128)} %get-tuple-element.11.sums), custom_call_target="tpu_custom_call" | custom-call | tf_op jit(solution)/shard_map/pallas_call | solution.py:1191

commit v4 on v3

--- a/solution.py
+++ b/solution.py
@@ -437,8 +437,8 @@
 BLOCKS = (WIN - 4) // BLOCK
 ROWS = BLOCK * 8
 HALF = ROWS // 2
-PIECES = ((0, 2), (2, 6), (8, 6), (14, 4), (18, 2))
-ARRIVE = ((0, 1), (2,), (3, 4))
+PIECES = ((0, 8), (8, 6), (14, 6))
+RETURNS = ((0, 4), (4, 6), (10, 6))
 WANTED = 38
 HIGH = lax.Precision.HIGHEST
 
@@ -468,7 +468,7 @@
     field, odd, smooth, gwall, gsm, godd, hid, slope, part_out, part_in,
     taps, fore, wide, wide_t, band_tile, wall, wall_acc, acc, gram, params, classes, classes_t,
     gout, mine, red,
-    in_sem, f_send, f_recv, l_send, l_recv, p_send, p_recv, g_send, g_recv, r_send, r_recv,
+    in_sem, own_sem, f_send, f_recv, l_send, l_recv, p_send, p_recv, g_send, g_recv, r_send, r_recv,
 ):
     size, depth, volume = dims
     everyone = size * depth * 2
@@ -485,26 +485,29 @@
     ins = [
         pltpu.make_async_copy(src, dst, in_sem.at[n])
         for n, (src, dst) in enumerate((
-            (feat_h, feat), (lab_h, lab), (index_h, index), (stretch_h, stretch),
+            (feat_h.at[pl.ds(0, 16)], feat.at[pl.ds(0, 16)]),
+            (feat_h.at[pl.ds(16, 16)], feat.at[pl.ds(16, 16)]),
+            (lab_h, lab), (index_h, index), (stretch_h, stretch),
             (tile_h, tile_w), (wall_h, wall_w), (class_h, class_w),
         ))
     ]
     for copy in ins:
         copy.start()
 
-    def coords(step):
-        place = lax.rem(me + step, everyone)
-        return {
-            "gx": place // (2 * depth),
-            "gz": lax.rem(place // 2, depth),
-            "col": lax.rem(place, 2),
-        }
+    gx_at = [lax.rem(gx + n, size) for n in range(size)]
+    gz_at = [lax.rem(gz + n, depth) for n in range(depth)]
+    col_at = [col, 1 - col]
+    steps = [
+        (sx, sz, sc)
+        for sx in range(size) for sz in range(depth) for sc in range(2) if sx or sz or sc
+    ]
+
+    def coords(sx, sz, sc):
+        return {"gx": gx_at[sx], "gz": gz_at[sz], "col": col_at[sc]}
 
     barrier = pltpu.get_barrier_semaphore()
-
-    @pl.loop(1, everyone)
-    def _(step):
-        pl.semaphore_signal(barrier, inc=1, device_id=coords(step), device_id_type=MESH)
+    for step in steps:
+        pl.semaphore_signal(barrier, inc=1, device_id=coords(*step), device_id_type=MESH)
 
     def remote(src, dst, sent, got, device):
         return pltpu.make_async_remote_copy(
@@ -513,127 +516,158 @@
         )
 
     def target(sx):
-        return lax.rem(gx + sx, size)
+        return gx_at[sx] if isinstance(sx, int) else lax.rem(gx + sx, size)
 
     def origin(sx):
-        return lax.rem(gx + size - sx, size)
-
-    ins[0].wait()
-    for side in range(2):
+        return gx_at[-sx % size]
+
+    def turned_features(side):
+        ins[side].wait()
         for cp in range(8):
             block = feat[pl.ds(side * 16 + 2 * cp, 2)].astype(F32).reshape(128, 128)
             turn[side, pl.ds(cp, 128, stride=8), :] = block.T
 
         @pl.loop(0, 64, unroll=8)
-        def _(zp, side=side):
+        def _(zp):
             at = pl.ds(pl.multiple_of(zp * 16, 16), 16)
             send[side, zp] = turn[side, at, :].astype(BF16)
 
-    ins[1].wait()
+    last = len(PIECES) - 1
+
+    def f_copy(piece, sx, ct, part, way):
+        t, sc = target(sx), col_at[ct] if isinstance(ct, int) else 0
+        at, count = part
+        return remote(
+            send.at[ct, pl.ds(lax.rem(t * zps + at - 2 + 64, 64), count)],
+            recv.at[gx, col, pl.ds(at, count)],
+            f_send.at[piece, sx, sc], f_recv.at[piece, sx, sc],
+            {"gx": t, "gz": gz_at[way % depth], "col": ct},
+        )
+
+    def edge_part(piece):
+        at, count = PIECES[piece]
+        return ((at, 2), (at + 2, count - 2)) if piece == 0 else (
+            (at + count - 2, 2), (at, count - 2)
+        )
+
+    def f_start(piece, sx, ct):
+        t = target(sx)
+        if 0 < piece < last:
+            f_copy(piece, sx, ct, PIECES[piece], 0).start()
+            return
+        end, way = (0, 1) if piece == 0 else (size - 1, -1)
+        far, near = edge_part(piece)
+
+        @pl.when(t != end)
+        def _():
+            f_copy(piece, sx, ct, PIECES[piece], 0).start()
+
+        @pl.when(t == end)
+        def _():
+            f_copy(piece, sx, ct, near, 0).start()
+            f_copy(piece, sx, ct, far, way).start()
+
+    def f_own(piece, part):
+        at, count = part
+        return pltpu.make_async_copy(
+            send.at[col, pl.ds(lax.rem(gx * zps + at - 2 + 64, 64), count)],
+            recv.at[gx, col, pl.ds(at, count)], own_sem.at[piece],
+        )
+
+    def own_piece(piece, whole_one, near_one, far_one):
+        if 0 < piece < last:
+            whole_one(f_own(piece, PIECES[piece]))
+            return
+        end, way = (0, 1) if piece == 0 else (size - 1, -1)
+        far, near = edge_part(piece)
+
+        @pl.when(gx != end)
+        def _():
+            whole_one(f_own(piece, PIECES[piece]))
+
+        @pl.when(gx == end)
+        def _():
+            near_one(f_own(piece, near))
+            far_one(f_copy(piece, 0, col, far, way))
+
+    def begin(copy):
+        copy.start()
+
+    def f_send_all(piece, ct):
+        for sx in (2, 1, 3):
+            f_start(piece, sx, ct)
+
+        @pl.when(col != ct)
+        def _():
+            f_start(piece, 0, ct)
+
+        @pl.when(col == ct)
+        def _():
+            own_piece(piece, begin, begin, begin)
+
+    others = [(sx, sc) for sx in (2, 1, 3, 0) for sc in range(2) if sx or sc]
+
+    def f_wait(piece, sx, sc):
+        slot = recv.at[origin(sx), col_at[sc], pl.ds(*PIECES[piece])]
+        return remote(
+            slot, slot, f_send.at[piece, sx, sc], f_recv.at[piece, sx, sc],
+            {"gx": target(sx), "gz": gz, "col": col_at[sc]},
+        )
+
+    turned_features(0)
+    pl.semaphore_wait(barrier, everyone - 1)
+    f_send_all(0, 0)
+    turned_features(1)
+    f_send_all(0, 1)
+
+    ins[2].wait()
     turn[2, 0:128, :] = lab[...].astype(F32).T
     even, uneven = turn[2, pl.ds(0, 64, stride=2), :], turn[2, pl.ds(1, 64, stride=2), :]
     here = jnp.where(col == 0, even, pltpu.roll(even, 64, 1))
     there = jnp.where(col == 0, pltpu.roll(uneven, 64, 1), uneven)
     lab_rows[...] = jnp.where(lax.broadcasted_iota(jnp.int32, (64, 128), 1) < 64, here, there)
-    for t in range(size):
-        lab_send[t] = lab_rows[pl.ds(zps * t, zps), :].astype(BF16)
     edge_rows = [jnp.zeros((1, 128), F32)] * 16
     for t in range(size):
         edge_rows[2 * t] = lab_rows[pl.ds((zps * t - 1) % 64, 1), :]
         edge_rows[2 * t + 1] = lab_rows[pl.ds((zps * t + zps) % 64, 1), :]
-    lab_send[size] = jnp.concatenate(edge_rows, axis=0).astype(BF16)
-
-    pl.semaphore_wait(barrier, everyone - 1)
-
-    def f_spot(piece, t):
-        at, count = PIECES[piece]
-        return pl.ds(lax.rem(t * zps + at - 2 + 64, 64), count), pl.ds(at, count)
-
-    def f_far(piece, sx, sc):
-        t, ct = target(sx), lax.rem(col + sc, 2)
-        src, dst = f_spot(piece, t)
-        if piece == 0:
-            tz = lax.rem(gz + 1 - (t + size - 1) // size, depth)
-        elif piece == len(PIECES) - 1:
-            tz = lax.rem(gz + depth - (t + 1) // size, depth)
-        else:
-            tz = gz
+    edge_rows = jnp.concatenate(edge_rows, axis=0).astype(BF16)
+    for t in range(size):
+        lab_send[t, 0] = lab_rows[pl.ds(zps * t, zps), :].astype(BF16)
+        lab_send[t, 1] = edge_rows
+
+    def l_copy(sx):
         return remote(
-            send.at[ct, src], recv.at[gx, col, dst],
-            f_send.at[piece, sx, sc], f_recv.at[piece, sx, sc],
-            {"gx": t, "gz": tz, "col": ct},
-        )
-
-    def f_near(piece):
-        src, dst = f_spot(piece, gx)
-        return pltpu.make_async_copy(
-            send.at[col, src], recv.at[gx, col, dst], f_recv.at[piece, 0, 0]
-        )
-
-    def f_wait(piece, sx, sc):
-        at, count = PIECES[piece]
-        slot = recv.at[origin(sx), lax.rem(col + sc, 2), pl.ds(at, count)]
+            lab_send.at[target(sx)], lab_recv.at[gx, pl.ds(0, 2)],
+            l_send.at[0, sx], l_recv.at[0, sx], {"gx": target(sx)},
+        )
+
+    def l_far(sx, way):
         return remote(
-            slot, slot, f_send.at[piece, sx, sc], f_recv.at[piece, sx, sc],
-            {"gx": target(sx), "gz": gz, "col": lax.rem(col + sc, 2)},
-        )
-
-    def own_piece(piece, near, far):
-        if piece == 0:
-            pl.when(gx > 0)(near)
-            pl.when(gx == 0)(far)
-        elif piece == len(PIECES) - 1:
-            pl.when(gx < size - 1)(near)
-            pl.when(gx == size - 1)(far)
-        else:
-            near()
-
-    others = [(sx, sc) for sx in (2, 1, 3, 0) for sc in range(2) if sx or sc]
-
-    def l_mid(sx):
-        return remote(
-            lab_send.at[target(sx)], lab_recv.at[gx, 0], l_send.at[0, sx], l_recv.at[0, sx],
-            {"gx": target(sx)},
-        )
-
-    def l_edge(sx):
-        return remote(
-            lab_send.at[size], lab_recv.at[gx, 1], l_send.at[1, sx], l_recv.at[1, sx],
-            {"gx": target(sx)},
-        )
-
-    def l_far(sx):
-        t = target(sx)
-        tz = lax.rem(gz + depth + 1 - 2 * ((t + 1) // size), depth)
-        return remote(
-            lab_send.at[size], lab_recv.at[gx, 2], l_send.at[2, sx], l_recv.at[2, sx],
-            {"gx": t, "gz": tz},
-        )
-
-    l_own = [
-        pltpu.make_async_copy(lab_send.at[gx], lab_recv.at[gx, 0], l_recv.at[0, 0]),
-        pltpu.make_async_copy(lab_send.at[size], lab_recv.at[gx, 1], l_recv.at[1, 0]),
-    ]
-
-    for block in range(BLOCKS):
-        for piece in ARRIVE[block]:
-            for sx, sc in others:
-                f_far(piece, sx, sc).start()
-            own_piece(
-                piece,
-                lambda piece=piece: f_near(piece).start(),
-                lambda piece=piece: f_far(piece, 0, 0).start(),
-            )
-        if block == 0:
-            for copy in l_own:
-                copy.start()
-            for sx in range(size):
-                if sx:
-                    l_mid(sx).start()
-                    l_edge(sx).start()
-                l_far(sx).start()
-
-    for copy in ins[2:]:
+            lab_send.at[target(sx), 1], lab_recv.at[gx, 2], l_send.at[1, sx], l_recv.at[1, sx],
+            {"gx": target(sx), "gz": gz_at[way % depth]},
+        )
+
+    l_own = pltpu.make_async_copy(lab_send.at[gx], lab_recv.at[gx, pl.ds(0, 2)], own_sem.at[3])
+    l_own.start()
+
+    def at_ends(sx, act):
+        @pl.when(target(sx) == 0)
+        def _():
+            act(l_far(sx, 1))
+
+        @pl.when(target(sx) == size - 1)
+        def _():
+            act(l_far(sx, -1))
+
+    for sx in range(size):
+        if sx:
+            l_copy(sx).start()
+        at_ends(sx, begin)
+    for piece in range(1, len(PIECES)):
+        for ct in range(2):
+            f_send_all(piece, ct)
+
+    for copy in ins[3:]:
         copy.wait()
     params[...] = jnp.zeros((128, 128), F32)
     params[0:9, 0:32] = wall_w[...]
@@ -717,15 +751,12 @@
     classes_t[...] = classes[...].T
 
     def arrived(block):
-        for piece in ARRIVE[block]:
-            for sx, sc in others:
-                f_wait(piece, sx, sc).wait_recv()
-            own_piece(
-                piece,
-                lambda piece=piece: f_near(piece).wait(),
-                lambda piece=piece: f_wait(piece, 0, 0).wait_recv(),
-            )
-        low, high = PIECES[ARRIVE[block][0]][0], sum(PIECES[ARRIVE[block][-1]])
+        for sx, sc in others:
+            f_wait(block, sx, sc).wait_recv()
+        own_piece(
+            block, lambda copy: copy.wait(), lambda copy: copy.wait(), lambda copy: copy.wait_recv()
+        )
+        low, high = PIECES[block][0], sum(PIECES[block])
 
         @pl.loop(0, 2 * size)
         def _(t):
@@ -868,32 +899,29 @@
         low = 4 if block == 0 else BLOCK * block
         return low, BLOCK * block + BLOCK - low
 
-    def g_copy(block, step):
-        low, count = g_spot(block)
-        at, many = (low - 4) // 2, count // 2
+    def g_copy(back, step):
+        at, many = RETURNS[back]
         p, yh = target(step // 2), lax.rem(col + step, 2)
         return remote(
             gout.at[2 * p + yh, pl.ds(at, many)],
             ghome.at[col, pl.ds(gx * zps + at, many)],
-            g_send.at[block, step], g_recv.at[block, step], {"gx": p, "col": yh},
-        )
-
-    def g_near(block):
-        low, count = g_spot(block)
-        at, many = (low - 4) // 2, count // 2
+            g_send.at[back, step], g_recv.at[back, step], {"gx": p, "col": yh},
+        )
+
+    def g_near(back):
+        at, many = RETURNS[back]
         return pltpu.make_async_copy(
             gout.at[2 * gx + col, pl.ds(at, many)],
             ghome.at[col, pl.ds(gx * zps + at, many)],
-            g_recv.at[block, 0],
-        )
-
-    def g_wait(block, step):
-        low, count = g_spot(block)
-        at, many = (low - 4) // 2, count // 2
-        slot = ghome.at[lax.rem(col + step, 2), pl.ds(origin(step // 2) * zps + at, many)]
+            g_recv.at[back, 0],
+        )
+
+    def g_wait(back, step):
+        at, many = RETURNS[back]
+        slot = ghome.at[col_at[step % 2], pl.ds(origin(step // 2) * zps + at, many)]
         return remote(
-            slot, slot, g_send.at[block, step], g_recv.at[block, step],
-            {"gx": target(step // 2), "col": lax.rem(col + step, 2)},
+            slot, slot, g_send.at[back, step], g_recv.at[back, step],
+            {"gx": target(step // 2), "col": col_at[step % 2]},
         )
 
     def home(block):
@@ -920,35 +948,38 @@
                 g_near(block).start()
 
     def labels_in():
+        at_end = (gx == 0) | (gx == size - 1)
         for sx in range(size):
             if sx:
-                for slot in range(2):
-                    at = lab_recv.at[origin(sx), slot]
-                    remote(
-                        at, at, l_send.at[slot, sx], l_recv.at[slot, sx], {"gx": target(sx)}
-                    ).wait_recv()
-            at = lab_recv.at[origin(sx), 2]
-            remote(
-                at, at, l_send.at[2, sx], l_recv.at[2, sx], {"gx": target(sx), "gz": right}
-            ).wait_recv()
-        for copy in l_own:
-            copy.wait()
+                at = lab_recv.at[origin(sx), pl.ds(0, 2)]
+                remote(
+                    at, at, l_send.at[0, sx], l_recv.at[0, sx], {"gx": target(sx)}
+                ).wait_recv()
+
+            @pl.when(at_end)
+            def _(sx=sx):
+                at = lab_recv.at[origin(sx), 2]
+                remote(
+                    at, at, l_send.at[1, sx], l_recv.at[1, sx], {"gx": target(sx), "gz": right}
+                ).wait_recv()
+                lab_wide[origin(sx), 2] = lab_recv[origin(sx), 2].astype(F32)
+
+        l_own.wait()
         low_edge = 2 - (gx + size - 1) // size
         high_edge = 1 + (gx + 1) // size
         for p in range(size):
             lab_win[p, 1 : 1 + zps, :] = lab_recv[p, 0].astype(F32)
-            for slot in range(1, 3):
-                lab_wide[p, slot] = lab_recv[p, slot].astype(F32)
+            lab_wide[p, 1] = lab_recv[p, 1].astype(F32)
             lab_win[p, 0:1, :] = lab_wide[p, low_edge, pl.ds(2 * gx, 1), :]
             lab_win[p, 1 + zps : 2 + zps, :] = lab_wide[p, high_edge, pl.ds(2 * gx + 1, 1), :]
 
     arrived(0)
     labels_in()
     ahead_of(0)
+    back_of(0)
+    home(0)
     arrived(1)
     ahead_of(1)
-    back_of(0)
-    home(0)
     arrived(2)
     ahead_of(2)
     back_of(1)
@@ -1038,50 +1069,43 @@
         total = total + dot(by_lane, place.astype(F32))
     mine[...] = total
 
-    def r_copy(step):
-        return remote(mine, sums.at[me], r_send.at[step], r_recv.at[step], coords(step))
+    def r_copy(n):
+        return remote(mine, sums.at[me], r_send.at[n + 1], r_recv.at[n + 1], coords(*steps[n]))
 
     r_own = pltpu.make_async_copy(mine, sums.at[me], r_recv.at[0])
     r_own.start()
 
-    @pl.loop(1, everyone)
-    def _(step):
-        r_copy(step).start()
-
-    for block in range(BLOCKS):
+    for n in range(len(steps)):
+        r_copy(n).start()
+
+    for back in range(BLOCKS):
         for step in range(1, 2 * size):
-            g_wait(block, step).wait_recv()
-        g_near(block).wait()
-
-    def r_wait(step):
-        place = lax.rem(me + everyone - step, everyone)
-        return remote(
-            sums.at[place], sums.at[place], r_send.at[step], r_recv.at[step], coords(step)
-        )
-
-    @pl.loop(1, everyone)
-    def _(step):
-        r_wait(step).wait_recv()
-
+            g_wait(back, step).wait_recv()
+        g_near(back).wait()
+
+    for n, (sx, sz, sc) in enumerate(steps):
+        place = (origin(sx) * depth + gz_at[-sz % depth]) * 2 + col_at[sc]
+        remote(
+            sums.at[place], sums.at[place], r_send.at[n + 1], r_recv.at[n + 1], coords(sx, sz, sc)
+        ).wait_recv()
     r_own.wait()
     for piece in range(len(PIECES)):
         for sx, sc in others:
-            f_far(piece, sx, sc).wait_send()
-    pl.when(gx == 0)(lambda: f_far(0, 0, 0).wait_send())
-    pl.when(gx == size - 1)(lambda: f_far(len(PIECES) - 1, 0, 0).wait_send())
+            f_wait(piece, sx, sc).wait_send()
+    pl.when(gx == 0)(lambda: f_copy(0, 0, col, edge_part(0)[0], 1).wait_send())
+    pl.when(gx == size - 1)(lambda: f_copy(last, 0, col, edge_part(last)[0], -1).wait_send())
     for sx in range(size):
         if sx:
-            l_mid(sx).wait_send()
-            l_edge(sx).wait_send()
-        l_far(sx).wait_send()
+            l_copy(sx).wait_send()
+        at_ends(sx, lambda copy: copy.wait_send())
     for block in range(BLOCKS):
         p_copy(block).wait_send()
+    for back in range(BLOCKS):
         for step in range(1, 2 * size):
-            g_copy(block, step).wait_send()
-
-    @pl.loop(1, everyone)
-    def _(step):
-        r_copy(step).wait_send()
+            g_copy(back, step).wait_send()
+
+    for n in range(len(steps)):
+        r_copy(n).wait_send()
 
 
 def last_kernel(volume, home, sums, out, tile_out, wall_out, class_out, turn, red):
@@ -1150,7 +1174,7 @@
             pltpu.VMEM((2, 64, 16, 128), BF16),
             pltpu.VMEM((size, 2, WIN // 2, 16, 128), BF16),
             pltpu.VMEM((64, 128), F32),
-            pltpu.VMEM((size + 1, 16, 128), BF16),
+            pltpu.VMEM((size, 2, 16, 128), BF16),
             pltpu.VMEM((size, 3, 16, 128), BF16),
             pltpu.VMEM((size, 3, 16, 128), F32),
             pltpu.VMEM((size, 24, 128), F32),
@@ -1171,9 +1195,9 @@
             pltpu.VMEM((2 * size, OWN // 2, 16, 128), BF16),
             pltpu.VMEM((8, 128), F32),
             pltpu.VMEM((128, 128), F32),
-            dma((7,)),
+            dma((8,)), dma((4,)),
             dma((len(PIECES), size, 2)), dma((len(PIECES), size, 2)),
-            dma((3, size)), dma((3, size)),
+            dma((2, size)), dma((2, size)),
             dma((BLOCKS,)), dma((BLOCKS,)),
             dma((BLOCKS, 2 * size)), dma((BLOCKS, 2 * size)),
             dma((everyone,)), dma((everyone,)),

time: 47 us -> 45.5 us (0.968)
  Pallas kernels: 46.2 us -> 44.7 us
    pallas_call x1, Pallas kernels: 43.7 us -> 42.3 us  [regional(): pl.pallas_call(functools.partial(region_kernel, (size, depth, volume)), o...]
where the time goes in v4:
time: 45.5 us; the launch traced here: 45.4 us
  Pallas kernels  44.7 us (98%)
  between operations  0.64 us (1%)
    pallas_call x1, Pallas kernels, regional(): pl.pallas_call(functools.partial(region_kernel, (size, depth, volume)), o...  42.3 us
    pallas_call x1, Pallas kernels, regional(): pl.pallas_call(functools.partial(last_kernel, volume), grid=(2,), out_sha...  2.46 us

profile of v4, /device:TPU:0, one launch (start us, length us, event | category | flops | bytes accessed | tf_op | source)
XLA Modules:
  0.0 45.4 jit_solution(3235417531674525738)
XLA Ops:
  0.6 42.3 %shard_map.102 = (bf16[2,64,16,128]{3,2,1,0:T(8,128)(2,1)}, f32[16,8,128]{2,1,0:T(8,128)}) custom-call(bf16[32,64,128]{2,1,0:T(8,128)(2,1)} %bitcast.6, s32[128,128]{1,0:T(8,128)} %bitcast.7, s32[1,64]{1,0:T(1,128)} %bitcast.9, f32[16,9]{1,0:T(8,128)} %stretch_h.1, f32[32,25]{1,0:T(8,128)} %tile_h.1, f32[9,32]{1,0:T(8,128)} %bitcast.8, f32[4,32]{1,0:T(4,128)} %class_h.1), custom_call_target="tpu_custom_call" | custom-call | tf_op jit(solution)/shard_map/pallas_call | solution.py:1157
  42.9 2.5 %shard_map.103 = (bf16[32,64,128]{2,1,0:T(8,128)(2,1)}, f32[32,25]{1,0:T(8,128)}, f32[9,32]{1,0:T(8,128)}, f32[4,32]{1,0:T(4,128)}) custom-call(bf16[2,64,16,128]{3,2,1,0:T(8,128)(2,1)} %get-tuple-element.10.home, f32[16,8,128]{2,1,0:T(8,128)} %get-tuple-element.11.sums), custom_call_target="tpu_custom_call" | custom-call | tf_op jit(solution)/shard_map/pallas_call | solution.py:1215

commit v5 on v4

--- a/solution.py
+++ b/solution.py
@@ -663,9 +663,6 @@
         if sx:
             l_copy(sx).start()
         at_ends(sx, begin)
-    for piece in range(1, len(PIECES)):
-        for ct in range(2):
-            f_send_all(piece, ct)
 
     for copy in ins[3:]:
         copy.wait()
@@ -973,13 +970,21 @@
             lab_win[p, 0:1, :] = lab_wide[p, low_edge, pl.ds(2 * gx, 1), :]
             lab_win[p, 1 + zps : 2 + zps, :] = lab_wide[p, high_edge, pl.ds(2 * gx + 1, 1), :]
 
+    def next_piece(piece):
+        for sx, sc in others:
+            f_wait(piece - 1, sx, sc).wait_send()
+        for ct in range(2):
+            f_send_all(piece, ct)
+
+    next_piece(1)
     arrived(0)
     labels_in()
     ahead_of(0)
+    next_piece(2)
+    arrived(1)
+    ahead_of(1)
     back_of(0)
     home(0)
-    arrived(1)
-    ahead_of(1)
     arrived(2)
     ahead_of(2)
     back_of(1)
@@ -1089,7 +1094,7 @@
             sums.at[place], sums.at[place], r_send.at[n + 1], r_recv.at[n + 1], coords(sx, sz, sc)
         ).wait_recv()
     r_own.wait()
-    for piece in range(len(PIECES)):
+    for piece in (2,):
         for sx, sc in others:
             f_wait(piece, sx, sc).wait_send()
     pl.when(gx == 0)(lambda: f_copy(0, 0, col, edge_part(0)[0], 1).wait_send())
@@ -1109,36 +1114,34 @@
 
 
 def last_kernel(volume, home, sums, out, tile_out, wall_out, class_out, turn, red):
-    side = pl.program_id(0)
     members = sums.shape[0] // 2
 
-    @pl.loop(0, 64, unroll=8)
-    def _(zp):
-        at = pl.ds(pl.multiple_of(zp * 16, 16), 16)
-        turn[at, :] = home[0, zp].astype(F32)
-
-    for cp in range(8):
-        block = turn[pl.ds(cp, 128, stride=8), :].T
+    for side in range(2):
+        @pl.loop(0, 64, unroll=8)
+        def _(zp, side=side):
+            at = pl.ds(pl.multiple_of(side * 1024 + zp * 16, 16), 16)
+            turn[at, :] = home[side, zp].astype(F32)
+
+    for cp in range(16):
+        block = turn[pl.ds(cp // 8 * 1024 + cp % 8, 128, stride=8), :].T
         out[pl.ds(2 * cp, 2)] = block.reshape(2, 64, 128).astype(BF16)
 
-    @pl.when(side == 0)
-    def _():
-        spot = lax.broadcasted_iota(jnp.int32, (128, 128), 0)
-        want = 2 * lax.broadcasted_iota(jnp.int32, (128, 128), 1)
-        red[...] = jnp.zeros((128, 128), F32)
-        for half in range(2):
-            total = sums[half]
-            for member in range(1, members):
-                total = total + sums[2 * member + half]
-            total = total / volume
-            for par in range(2):
-                red[pl.ds(half * 16 + par, 8, stride=2), :] = dot(
-                    total, (spot == want + par).astype(F32)
-                )
-        turned = red[...].T
-        tile_out[...] = red[0:32, 0:25]
-        wall_out[...] = turned[25:34, 0:32]
-        class_out[...] = turned[34:38, 0:32]
+    spot = lax.broadcasted_iota(jnp.int32, (128, 128), 0)
+    want = 2 * lax.broadcasted_iota(jnp.int32, (128, 128), 1)
+    red[...] = jnp.zeros((128, 128), F32)
+    for half in range(2):
+        total = sums[half]
+        for member in range(1, members):
+            total = total + sums[2 * member + half]
+        total = total / volume
+        for par in range(2):
+            red[pl.ds(half * 16 + par, 8, stride=2), :] = dot(
+                total, (spot == want + par).astype(F32)
+            )
+    turned = red[...].T
+    tile_out[...] = red[0:32, 0:25]
+    wall_out[...] = turned[25:34, 0:32]
+    class_out[...] = turned[34:38, 0:32]
 
 
 def regional(
@@ -1210,11 +1213,10 @@
         stretch, tile_filter, wall_filter.T, class_weight,
     )
     def whole(*shape):
-        return pl.BlockSpec(shape, lambda side: (0,) * len(shape))
+        return pl.BlockSpec(shape, lambda: (0,) * len(shape))
 
     grad, tile_grad, wall_grad, class_grad = pl.pallas_call(
         functools.partial(last_kernel, volume),
-        grid=(2,),
         out_shape=(
             jax.ShapeDtypeStruct((chans, 64, 128), BF16),
             jax.ShapeDtypeStruct((chans, 25), F32),
@@ -1222,14 +1224,14 @@
             jax.ShapeDtypeStruct((4, chans), F32),
         ),
         in_specs=[
-            pl.BlockSpec((1, 64, 16, 128), lambda side: (side, 0, 0, 0)),
+            whole(2, 64, 16, 128),
             whole(everyone, 8, 128),
         ],
         out_specs=(
-            pl.BlockSpec((chans // 2, 64, 128), lambda side: (side, 0, 0)),
+            whole(chans, 64, 128),
             whole(chans, 25), whole(9, chans), whole(4, chans),
         ),
-        scratch_shapes=[pltpu.VMEM((1024, 128), F32), pltpu.VMEM((128, 128), F32)],
+        scratch_shapes=[pltpu.VMEM((2048, 128), F32), pltpu.VMEM((128, 128), F32)],
     )(home, sums)
     return grad.reshape(features.shape), tile_grad, wall_grad.T, class_grad
 

time: 45.5 us -> 44.5 us (0.978)
  Pallas kernels: 44.7 us -> 43.7 us
    pallas_call x1, Pallas kernels: 42.3 us -> 41.4 us  [regional(): pl.pallas_call(functools.partial(region_kernel, (size, depth, volume)), o...]
where the time goes in v5:
time: 44.5 us; the launch traced here: 44.4 us
  Pallas kernels  43.7 us (98%)
  between operations  0.64 us (1%)
    pallas_call x1, Pallas kernels, regional(): pl.pallas_call(functools.partial(region_kernel, (size, depth, volume)), o...  41.4 us
    pallas_call x1, Pallas kernels, regional(): pl.pallas_call(functools.partial(last_kernel, volume), out_shape=(jax.Sha...  2.3 us

profile of v5, /device:TPU:0, one launch (start us, length us, event | category | flops | bytes accessed | tf_op | source)
XLA Modules:
  0.0 44.4 jit_solution(9782732693306723828)
XLA Ops:
  0.6 41.4 %shard_map.102 = (bf16[2,64,16,128]{3,2,1,0:T(8,128)(2,1)}, f32[16,8,128]{2,1,0:T(8,128)}) custom-call(bf16[32,64,128]{2,1,0:T(8,128)(2,1)} %bitcast.6, s32[128,128]{1,0:T(8,128)} %bitcast.7, s32[1,64]{1,0:T(1,128)} %bitcast.9, f32[16,9]{1,0:T(8,128)} %stretch_h.1, f32[32,25]{1,0:T(8,128)} %tile_h.1, f32[9,32]{1,0:T(8,128)} %bitcast.8, f32[4,32]{1,0:T(4,128)} %class_h.1), custom_call_target="tpu_custom_call" | custom-call | tf_op jit(solution)/shard_map/pallas_call | solution.py:1160
  42.1 2.3 %shard_map.103 = (bf16[32,64,128]{2,1,0:T(8,128)(2,1)}, f32[32,25]{1,0:T(8,128)}, f32[9,32]{1,0:T(8,128)}, f32[4,32]{1,0:T(4,128)}) custom-call(bf16[2,64,16,128]{3,2,1,0:T(8,128)(2,1)} %get-tuple-element.10.home, f32[16,8,128]{2,1,0:T(8,128)} %get-tuple-element.11.sums), custom_call_target="tpu_custom_call" | custom-call | tf_op jit(solution)/shard_map/pallas_call | solution.py:1218

commit v6 on v5

--- a/solution.py
+++ b/solution.py
@@ -771,13 +771,17 @@
         return lambda t, z: ref[lax.rem(t, 2), spot(z, t // 2), :]
 
     def between(src, dst, low, high):
-        @pl.loop(0, 2 * size)
+        partner = square_lane + 1 - 2 * lax.rem(square_lane, 2)
+        swap = (square_row == partner).astype(F32).astype(BF16)
+
+        @pl.loop(0, 2 * size, unroll=4)
         def _(t):
             after = lax.rem(t + 2, 2 * size)
+            mixed = [jnp.where(x_even, src(after, z), src(t, z)) for z in range(low, high)]
+            mixed = jnp.concatenate(mixed, axis=0).astype(BF16)
+            swapped = jnp.dot(mixed, swap, preferred_element_type=F32)
             for z in range(low, high):
-                dst[t, z] = jnp.where(
-                    x_even, pltpu.roll(src(t, z), 127, 1), pltpu.roll(src(after, z), 1, 1)
-                )
+                dst[t, z] = swapped[8 * (z - low) : 8 * (z - low) + 8]
 
     def filtered(src, mid, t, low, count, flip, put):
         before, after = lax.rem(t + 2 * size - 2, 2 * size), lax.rem(t + 2, 2 * size)

time: 44.5 us -> 43.4 us (0.975)
  Pallas kernels: 43.7 us -> 42.6 us
    pallas_call x1, Pallas kernels: 41.4 us -> 40.3 us  [regional(): pl.pallas_call(functools.partial(region_kernel, (size, depth, volume)), o...]
where the time goes in v6:
time: 43.4 us; the launch traced here: 43.2 us
  Pallas kernels  42.6 us (98%)
  between operations  0.64 us (1%)
    pallas_call x1, Pallas kernels, regional(): pl.pallas_call(functools.partial(region_kernel, (size, depth, volume)), o...  40.3 us
    pallas_call x1, Pallas kernels, regional(): pl.pallas_call(functools.partial(last_kernel, volume), out_shape=(jax.Sha...  2.3 us

profile of v6, /device:TPU:0, one launch (start us, length us, event | category | flops | bytes accessed | tf_op | source)
XLA Modules:
  0.0 43.2 jit_solution(11714933991880640086)
XLA Ops:
  0.6 40.3 %shard_map.102 = (bf16[2,64,16,128]{3,2,1,0:T(8,128)(2,1)}, f32[16,8,128]{2,1,0:T(8,128)}) custom-call(bf16[32,64,128]{2,1,0:T(8,128)(2,1)} %bitcast.6, s32[128,128]{1,0:T(8,128)} %bitcast.7, s32[1,64]{1,0:T(1,128)} %bitcast.9, f32[16,9]{1,0:T(8,128)} %stretch_h.1, f32[32,25]{1,0:T(8,128)} %tile_h.1, f32[9,32]{1,0:T(8,128)} %bitcast.8, f32[4,32]{1,0:T(4,128)} %class_h.1), custom_call_target="tpu_custom_call" | custom-call | tf_op jit(solution)/shard_map/pallas_call | solution.py:1164
  40.9 2.3 %shard_map.103 = (bf16[32,64,128]{2,1,0:T(8,128)(2,1)}, f32[32,25]{1,0:T(8,128)}, f32[9,32]{1,0:T(8,128)}, f32[4,32]{1,0:T(4,128)}) custom-call(bf16[2,64,16,128]{3,2,1,0:T(8,128)(2,1)} %get-tuple-element.10.home, f32[16,8,128]{2,1,0:T(8,128)} %get-tuple-element.11.sums), custom_call_target="tpu_custom_call" | custom-call | tf_op jit(solution)/shard_map/pallas_call | solution.py:1222

commit v7 on v6

--- a/solution.py
+++ b/solution.py
@@ -983,8 +983,8 @@
     next_piece(1)
     arrived(0)
     labels_in()
+    next_piece(2)
     ahead_of(0)
-    next_piece(2)
     arrived(1)
     ahead_of(1)
     back_of(0)

time: 43.4 us -> 42.3 us (0.975)
  Pallas kernels: 42.6 us -> 41.5 us
    pallas_call x1, Pallas kernels: 40.3 us -> 39.2 us  [regional(): pl.pallas_call(functools.partial(region_kernel, (size, depth, volume)), o...]
where the time goes in v7:
time: 42.3 us; the launch traced here: 42.2 us
  Pallas kernels  41.5 us (98%)
  between operations  0.64 us (2%)
    pallas_call x1, Pallas kernels, regional(): pl.pallas_call(functools.partial(region_kernel, (size, depth, volume)), o...  39.2 us
    pallas_call x1, Pallas kernels, regional(): pl.pallas_call(functools.partial(last_kernel, volume), out_shape=(jax.Sha...  2.3 us

profile of v7, /device:TPU:0, one launch (start us, length us, event | category | flops | bytes accessed | tf_op | source)
XLA Modules:
  0.0 42.2 jit_solution(3858256147749030931)
XLA Ops:
  0.6 39.2 %shard_map.102 = (bf16[2,64,16,128]{3,2,1,0:T(8,128)(2,1)}, f32[16,8,128]{2,1,0:T(8,128)}) custom-call(bf16[32,64,128]{2,1,0:T(8,128)(2,1)} %bitcast.6, s32[128,128]{1,0:T(8,128)} %bitcast.7, s32[1,64]{1,0:T(1,128)} %bitcast.9, f32[16,9]{1,0:T(8,128)} %stretch_h.1, f32[32,25]{1,0:T(8,128)} %tile_h.1, f32[9,32]{1,0:T(8,128)} %bitcast.8, f32[4,32]{1,0:T(4,128)} %class_h.1), custom_call_target="tpu_custom_call" | custom-call | tf_op jit(solution)/shard_map/pallas_call | solution.py:1164
  39.9 2.3 %shard_map.103 = (bf16[32,64,128]{2,1,0:T(8,128)(2,1)}, f32[32,25]{1,0:T(8,128)}, f32[9,32]{1,0:T(8,128)}, f32[4,32]{1,0:T(4,128)}) custom-call(bf16[2,64,16,128]{3,2,1,0:T(8,128)(2,1)} %get-tuple-element.10.home, f32[16,8,128]{2,1,0:T(8,128)} %get-tuple-element.11.sums), custom_call_target="tpu_custom_call" | custom-call | tf_op jit(solution)/shard_map/pallas_call | solution.py:1222
